TPU v7x, 512 devices: a whole 4x8x8 slice. The times are simulated.
512 devices in a mesh: dp: 16 (over z, core), seq: 32 (over y, x).
Axes of the slice: x: 4, y: 8, z: 8, core: 2. Of those that a mesh axis runs over, the one named last changes fastest.
Arguments:
- features: bfloat16 [16, 32, 128, 2560], P('dp', None, 'seq'), may hold values from -6 to 6
- frozen_query_weight: bfloat16 [16, 32, 128, 4096], P('dp', None, 'seq'), may hold values from -100 to 100
- source_keys: bfloat16 [16, 32, 128, 4096], P('dp', None, 'seq'), may hold values from -6 to 6
- source_values: bfloat16 [16, 32, 128, 4096], P('dp', None, 'seq'), may hold values from -6 to 6
- output_gradient: bfloat16 [16, 32, 128, 4096], P('dp', None, 'seq'), may hold values from -6 to 6
- adapter_down_weight: bfloat16 [2560, 64], replicated, may hold values from -0.125 to 0.125
- adapter_up_weight: bfloat16 [64, 4096], replicated, may hold values from -0.75 to 0.75
- source_block_plan: int32 [16, 32], replicated, may hold values from 0 to 511, as said below
- segments: int32 [16, 4096], P('dp'), may hold values from 0 to 1, never falling along the last dimension, each value on 1 to 2560 neighbouring positions
Outputs:
- down_grad: float32 [2560, 64], P('seq')
- up_grad: float32 [64, 4096], P(None, 'seq')
- log_norm: float32 [16, 32, 4096], P('dp', 'seq')
Inputs may be any that keep to these rules, and one draw needn't show every extreme that they name: `source_block_plan`: each entry names a source block as group * 32 + block; every source block is named exactly once; from one group to another group at most 2 blocks go, and some pairs of groups carry exactly 2. Within a group the segment numbers never fall and all 2 segments occur; a segment spans at most 2560 positions.
All inputs are finite; a program needn't handle non-finite values.
Results may differ from a plain program's by a relative error of at most 0.0087.
Values may be sent and summed in bfloat16 or wider, within the bound.
A program may use at most 64 MiB of HBM per device.

v0:
```python
import math

import jax
import jax.numpy as jnp
from jax import lax
from jax.sharding import PartitionSpec as P

CAP = 2
CLIPS = 2


def attend_head(query, key_rows, value_rows, cotangent, segment, clip_count, reach_rows):
    length = query.shape[0]
    width = query.shape[1]
    piece_count = 8
    piece_rows = reach_rows // piece_count
    scaling = 1.0 / math.sqrt(width)
    query_padded = jnp.pad(query, ((0, reach_rows), (0, 0)))
    grad_padded = jnp.pad(cotangent, ((0, reach_rows), (0, 0)))
    keys_padded = jnp.pad(key_rows, ((0, reach_rows), (0, 0)))
    values_padded = jnp.pad(value_rows, ((0, reach_rows), (0, 0)))
    segment_padded = jnp.pad(segment, (0, reach_rows), constant_values=-1)
    clip_ids = jnp.arange(clip_count, dtype=jnp.int32)
    starts = jnp.sum((segment[None, :] < clip_ids[:, None]).astype(jnp.int32), axis=1)

    def piece_pass(piece_index):
        clip_slice = piece_index // piece_count
        start = lax.dynamic_index_in_dim(starts, clip_slice, 0, keepdims=False)
        query_start = start + piece_index % piece_count * piece_rows
        query_tile = lax.dynamic_slice_in_dim(query_padded, query_start, piece_rows, 0)
        grad_tile = lax.dynamic_slice_in_dim(grad_padded, query_start, piece_rows, 0)
        seg_tile = lax.dynamic_slice_in_dim(segment_padded, query_start, piece_rows, 0)
        key_tile = lax.dynamic_slice_in_dim(keys_padded, start, reach_rows, 0)
        value_tile = lax.dynamic_slice_in_dim(values_padded, start, reach_rows, 0)
        seg_cols = lax.dynamic_slice_in_dim(segment_padded, start, reach_rows, 0)
        in_clip = seg_tile == clip_slice
        allowed = in_clip[:, None] & (seg_cols == clip_slice)[None, :]
        scores = (
            lax.dot_general(
                query_tile, key_tile, (((1,), (1,)), ((), ())), preferred_element_type=jnp.float32
            )
            * scaling
        )
        scores = jnp.where(allowed, scores, -1e30)
        maximum = jnp.max(scores, axis=1, keepdims=True)
        exponent = jnp.where(allowed, jnp.exp(scores - maximum), 0.0)
        totals = jnp.where(in_clip[:, None], jnp.sum(exponent, axis=1, keepdims=True), 1.0)
        log_norm = jnp.where(in_clip, maximum[:, 0] + jnp.log(totals[:, 0]), 0.0)
        probs = exponent / totals
        weights = probs.astype(jnp.bfloat16)
        attended = jnp.dot(weights, value_tile, preferred_element_type=jnp.float32)
        delta = jnp.sum(grad_tile.astype(jnp.float32) * attended, axis=1, keepdims=True)
        dprob = lax.dot_general(
            grad_tile, value_tile, (((1,), (1,)), ((), ())), preferred_element_type=jnp.float32
        )
        dscore = (probs * (dprob - delta)).astype(jnp.bfloat16)
        query_gradient = (
            jnp.dot(dscore, key_tile, preferred_element_type=jnp.float32) * scaling
        ).astype(jnp.bfloat16)
        query_gradient = jnp.where(in_clip[:, None], query_gradient, jnp.zeros((), jnp.bfloat16))
        return (query_gradient, log_norm, query_start)

    total_pieces = piece_count * (clip_count - 1)
    dquery_pieces, log_pieces, piece_starts = lax.map(
        piece_pass, jnp.arange(total_pieces, dtype=jnp.int32)
    )

    def place(index, carry):
        grad_total, log_total = carry
        where_at = lax.dynamic_index_in_dim(piece_starts, index, 0, keepdims=False)
        grad_piece = lax.dynamic_index_in_dim(dquery_pieces, index, 0, keepdims=False)
        log_piece = lax.dynamic_index_in_dim(log_pieces, index, 0, keepdims=False)
        grad_old = lax.dynamic_slice_in_dim(grad_total, where_at, piece_rows, 0)
        log_old = lax.dynamic_slice_in_dim(log_total, where_at, piece_rows, 0)
        grad_total = lax.dynamic_update_slice_in_dim(grad_total, grad_old + grad_piece, where_at, 0)
        log_total = lax.dynamic_update_slice_in_dim(log_total, log_old + log_piece, where_at, 0)
        return (grad_total, log_total)

    grad_init = jnp.zeros((length + reach_rows, width), jnp.bfloat16)
    log_init = jnp.zeros((length + reach_rows,), jnp.float32)
    grad_total, log_total = lax.fori_loop(0, total_pieces, place, (grad_init, log_init))
    return (grad_total[:length], log_total[:length])


def routing_tables(source_block_plan, group_index, cap_slots):
    group_count, block_count = source_block_plan.shape
    source_group = source_block_plan // block_count
    source_local = source_block_plan % block_count
    dest_groups = jnp.arange(group_count, dtype=jnp.int32)[:, None]
    outgoing = (source_group == group_index) & (dest_groups != group_index)
    out_rank = jnp.cumsum(outgoing.astype(jnp.int32), axis=1) - 1
    slot_ids = jnp.arange(cap_slots, dtype=jnp.int32)
    chosen = outgoing[:, :, None] & (out_rank[:, :, None] == slot_ids[None, None, :])
    send_index = jnp.sum(jnp.where(chosen, source_local[:, :, None], 0), axis=1)
    send_valid = jnp.any(chosen, axis=1)
    own_group = lax.dynamic_index_in_dim(source_group, group_index, 0, keepdims=False)
    own_local = lax.dynamic_index_in_dim(source_local, group_index, 0, keepdims=False)
    incoming = own_group != group_index
    positions = jnp.arange(block_count, dtype=jnp.int32)
    earlier = (own_group[None, :] == own_group[:, None]) & (positions[None, :] < positions[:, None])
    in_rank = jnp.sum(earlier.astype(jnp.int32), axis=1)
    return (send_index, send_valid, incoming, own_group, in_rank, own_local)


def pack_blocks(local, send_index, send_valid):
    picked = jnp.take(local, send_index, axis=0)
    return jnp.where(send_valid[:, :, None, None], picked, jnp.zeros((), local.dtype))


def unpack_blocks(received, local, tables, cap_slots):
    incoming, own_group, in_rank, own_local = tables
    flat = received.reshape((-1,) + received.shape[2:])
    slot_index = jnp.where(incoming, own_group * cap_slots + in_rank, 0)
    remote = jnp.take(flat, slot_index, axis=0)
    staying = jnp.take(local, own_local, axis=0)
    return jnp.where(incoming[:, None, None], remote, staying)


def per_device(
    features,
    frozen_query_weight,
    source_keys,
    source_values,
    output_gradient,
    adapter_down_weight,
    adapter_up_weight,
    source_block_plan,
    segments,
):
    group_count = lax.axis_size("dp")
    group_index = lax.axis_index("dp")
    block_count = features.shape[1]
    feat_local = features[0]
    base_local = frozen_query_weight[0]
    keys_local = source_keys[0]
    values_local = source_values[0]
    send_index, send_valid, incoming, own_group, in_rank, own_local = routing_tables(
        source_block_plan, group_index, CAP
    )
    tables = (incoming, own_group, in_rank, own_local)
    contract_final_axis = (((2,), (0,)), ((), ()))
    shuffled = (
        lax.all_to_all(
            pack_blocks(feat_local, send_index, send_valid),
            "dp",
            split_axis=0,
            concat_axis=0,
            tiled=True,
        ),
        lax.all_to_all(
            pack_blocks(base_local, send_index, send_valid),
            "dp",
            split_axis=0,
            concat_axis=0,
            tiled=True,
        ),
        lax.all_to_all(
            pack_blocks(keys_local, send_index, send_valid),
            "dp",
            split_axis=0,
            concat_axis=0,
            tiled=True,
        ),
        lax.all_to_all(
            pack_blocks(values_local, send_index, send_valid),
            "dp",
            split_axis=0,
            concat_axis=0,
            tiled=True,
        ),
    )
    feature_dest = unpack_blocks(shuffled[0], feat_local, tables, CAP)
    base_query_dest = unpack_blocks(shuffled[1], base_local, tables, CAP)
    keys_dest = unpack_blocks(shuffled[2], keys_local, tables, CAP)
    values_dest = unpack_blocks(shuffled[3], values_local, tables, CAP)
    adapter_params = lax.dot_general(
        feature_dest, adapter_down_weight, contract_final_axis, preferred_element_type=jnp.float32
    ).astype(jnp.bfloat16)
    query_rows = (
        base_query_dest.astype(jnp.float32)
        + lax.dot_general(
            adapter_params,
            adapter_up_weight,
            contract_final_axis,
            preferred_element_type=jnp.float32,
        )
    ).astype(jnp.bfloat16)
    head_query, head_keys, head_values, head_grads = (
        lax.all_to_all(query_rows, "seq", split_axis=2, concat_axis=1, tiled=True),
        lax.all_to_all(keys_dest, "seq", split_axis=2, concat_axis=1, tiled=True),
        lax.all_to_all(values_dest, "seq", split_axis=2, concat_axis=1, tiled=True),
        lax.all_to_all(output_gradient[0], "seq", split_axis=2, concat_axis=1, tiled=True),
    )
    length = head_query.shape[0] * head_query.shape[1]
    reach_rows = length // 2 + length // 8
    head_width = head_query.shape[2]
    segment = segments[0]
    head_query = head_query.reshape(length, head_width)
    head_keys = head_keys.reshape(length, head_width)
    head_values = head_values.reshape(length, head_width)
    head_grads = head_grads.reshape(length, head_width)
    dquery_head, log_head = attend_head(
        head_query, head_keys, head_values, head_grads, segment, CLIPS, reach_rows
    )
    norm_pieces = [log_head]
    log_norm = jnp.stack(norm_pieces, axis=0)
    query_gradient = lax.all_to_all(
        dquery_head.reshape(block_count, length // block_count, head_width),
        "seq",
        split_axis=1,
        concat_axis=2,
        tiled=True,
    )
    adapter_gradient = lax.dot_general(
        query_gradient,
        adapter_up_weight,
        (((2,), (1,)), ((), ())),
        preferred_element_type=jnp.float32,
    ).astype(jnp.bfloat16)
    contract_tokens = (((0, 1), (0, 1)), ((), ()))
    down_part = lax.dot_general(
        feature_dest, adapter_gradient, contract_tokens, preferred_element_type=jnp.float32
    )
    up_part = lax.dot_general(
        adapter_params, query_gradient, contract_tokens, preferred_element_type=jnp.float32
    )
    down_share, up_share = (
        lax.psum_scatter(down_part, "seq", scatter_dimension=0, tiled=True),
        lax.psum_scatter(up_part, "seq", scatter_dimension=1, tiled=True),
    )
    down_total, up_total = lax.psum((down_share, up_share), "dp")
    grad_norm = 4.0 / math.sqrt(group_count * length)
    return (down_total * grad_norm, up_total * grad_norm, log_norm[None])


def solution(mesh):
    in_specs = (
        P("dp", None, "seq", None),
        P("dp", None, "seq", None),
        P("dp", None, "seq", None),
        P("dp", None, "seq", None),
        P("dp", None, "seq", None),
        P(),
        P(),
        P(),
        P("dp", None),
    )
    out_specs = (P("seq", None), P(None, "seq"), P("dp", "seq", None))
    return jax.shard_map(
        per_device, mesh=mesh, in_specs=in_specs, out_specs=out_specs, check_vma=False
    )
```

profile of v0, /device:TPU:1, one launch (start us, length us, event | category | flops | bytes accessed | tf_op | source)
XLA Modules:
  0.0 1006.1 jit_solution(14845118212605083924)
XLA Ops:
  15.2 11.8 %all-to-all-start = ((bf16[16,2,4,2560]{3,2,1,0:T(4,128)(2,1)}), bf16[16,2,4,2560]{3,2,1,0:T(4,128)(2,1)}, u32[]{:S(2)}, u32[]{:S(2)}) async-start(bf16[16,2,4,2560]{3,2,1,0:T(4,128)(2,1)} %select_select_fusion.4), calls=%async_computation | async-start | bytes 1310720 | tf_op jit(solution)/shard_map/all_to_all | solution.py:143
  38.5 8.7 all-to-all-done
  47.1 31.6 %all_to_all.98 = bf16[16,2,4,4096]{3,2,1,0:T(4,128)(2,1)} all-to-all(bf16[16,2,4,4096]{3,2,1,0:T(4,128)(2,1)} %get-tuple-element.313), channel_id=1, replica_groups=mesh['dp'=16,'seq'=32] {'dp'}, dimensions={0} | all-to-all | bytes 2097152 | tf_op jit(solution)/shard_map/all_to_all | solution.py:157
  78.8 31.3 %all_to_all.99 = bf16[16,2,4,4096]{3,2,1,0:T(4,128)(2,1)} all-to-all(bf16[16,2,4,4096]{3,2,1,0:T(4,128)(2,1)S(1)} %get-tuple-element.312), channel_id=1, replica_groups=mesh['dp'=16,'seq'=32] {'dp'}, dimensions={0} | all-to-all | bytes 2097152 | tf_op jit(solution)/shard_map/all_to_all | solution.py:164
  113.6 7.2 copy.108
  126.2 7.6 reshape.258
  133.8 7.2 all-to-all-done.1
  142.0 9.8 all-to-all-start.5
  162.8 6.9 fusion.34
  174.4 7.7 reshape.256
  182.1 9.5 all-to-all-start.4
  196.3 7.6 reshape.260
  204.0 15.1 %all-to-all-done.4 = bf16[32,2,8192]{2,1,0:T(2,128)(2,1)S(1)} async-done(((bf16[32,2,8192]{2,1,0:T(2,128)(2,1)}), bf16[32,2,8192]{2,1,0:T(2,128)(2,1)S(1)}, u32[]{:S(2)}, u32[]{:S(2)}) %all-to-all-start.4) | async-done | bytes 1048608 | tf_op jit(solution)/shard_map/all_to_all | solution.py:190
  253.5 7.7 reshape.254
  261.1 9.3 all-to-all-start.2
  285.5 6.1 copy.107
  304.1 7.4 reshape.255
  311.4 6.1 copy.101
  318.9 125.3 %while.31 = (s32[]{:T(128)}, bf16[8,320,128]{2,1,0:T(8,128)(2,1)}, f32[8,320]{1,0:T(8,128)S(1)}, s32[8]{0:T(128)S(1)}, s32[8]{0:T(128)S(1)}, /*index=5*/s32[2]{0...) while((s32[]{:T(128)}, bf16[8,320,128]{2,1,0:T(8,128)(2,1)}, ...), condition=%wide.region_9.13_spmd, body=%wide.region_5.12_spmd.sunk | while | flops 852216960 | bytes 22656380 | solution.py:64
  444.5 32.6 %while.32 = (s32[]{:T(128)}, bf16[6656,128]{1,0:T(8,128)(2,1)S(1)}, f32[6656]{0:T(1024)S(1)}, s32[8]{0:T(128)S(1)}, bf16[8,320,128]{2,1,0:T(8,128)(2,1)}, /*inde...) while((s32[]{:T(128)}, bf16[6656,128]{1,0:T(8,128)(2,1)S(1)}, f32[6656]{0:T(1024)S(1)}, ...), condition=%wide.region_11.15_spmd, body=%wide.region_10.14_spmd.sunk | while | flops 164165 | bytes 418463 | solution.py:81
  477.8 33.4 %all_to_all.100 = bf16[32,128,128]{2,0,1:T(8,128)(2,1)S(1)} all-to-all(bf16[32,128,128]{2,0,1:T(8,128)(2,1)S(1)} %copy.116), channel_id=1, replica_groups=mesh['dp'=16,'seq'=32] {'seq'}, dimensions={1} | all-to-all | bytes 2097152 | tf_op jit(solution)/shard_map/all_to_all | solution.py:207
  515.3 210.3 %reduce-scatter.7.cloned.1.call-done = f32[80,64]{1,0:T(8,128)} async-done(((f32[2560,64]{1,0:T(8,128)}), f32[80,64]{1,0:T(8,128)}) %reduce-scatter.7.cloned.1.call-update) | async-done | bytes 20496
  726.5 221.4 %reduce-scatter.5.cloned.1.call-done = f32[64,128]{1,0:T(8,128)} async-done(((f32[64,4096]{1,0:T(8,128)}), f32[64,128]{1,0:T(8,128)}) %reduce-scatter.5.cloned.1.call-update) | async-done | bytes 32784 | tf_op jit(solution)/shard_map/reduce_scatter | solution.py:229
  947.9 49.7 %all-reduce.5 = (f32[80,64]{0,1:T(8,128)S(1)}, f32[64,128]{1,0:T(8,128)S(1)}) all-reduce(f32[80,64]{0,1:T(8,128)S(1)} %copy.120, f32[64,128]{1,0:T(8,128)} %reduce-scatter.5.cloned.1.call-done), channel_id=1, replica_groups=mesh['dp'=16,'seq'=32] {'dp'}, use_global_device_ids=true, to_apply=%region_13.17 | all-reduce | flops 13312 | bytes 106496 | tf_op jit(solution)/shard_map/psum | solution.py:231
  (242 shorter events, 220.3 us)
Async XLA Ops:
  7.2 22.4 %copy-start = (bf16[1,32,4,4096]{3,2,1,0:T(4,128)(2,1)S(1)}, bf16[1,32,4,4096]{3,2,1,0:T(4,128)(2,1)}, u32[]{:S(2)}) copy-start(bf16[1,32,4,4096]{3,2,1,0:T(4,128)(2,1)} %param.21) | copy-start | bytes 3145732
  7.2 20.0 %copy-start.3 = (bf16[1,32,4,4096]{3,2,1,0:T(4,128)(2,1)S(1)}, bf16[1,32,4,4096]{3,2,1,0:T(4,128)(2,1)}, u32[]{:S(2)}) copy-start(bf16[1,32,4,4096]{3,2,1,0:T(4,128)(2,1)} %param.20) | copy-start | bytes 3145732
  12.7 19.3 %copy-start.2 = (bf16[1,32,4,4096]{3,2,1,0:T(4,128)(2,1)S(1)}, bf16[1,32,4,4096]{3,2,1,0:T(4,128)(2,1)}, u32[]{:S(2)}) copy-start(bf16[1,32,4,4096]{3,2,1,0:T(4,128)(2,1)} %param.22) | copy-start | bytes 3145732
  15.2 32.0 %all-to-all-start = ((bf16[16,2,4,2560]{3,2,1,0:T(4,128)(2,1)}), bf16[16,2,4,2560]{3,2,1,0:T(4,128)(2,1)}, u32[]{:S(2)}, u32[]{:S(2)}) async-start(bf16[16,2,4,2560]{3,2,1,0:T(4,128)(2,1)} %select_select_fusion.4), calls=%async_computation | async-start | bytes 1310720 | tf_op jit(solution)/shard_map/all_to_all | solution.py:143
  110.1 30.9 %all-to-all-start.1 = ((bf16[16,2,4,4096]{3,2,1,0:T(4,128)(2,1)}), bf16[16,2,4,4096]{3,2,1,0:T(4,128)(2,1)S(1)}, u32[]{:S(2)}, u32[]{:S(2)}) async-start(bf16[16,2,4,4096]{3,2,1,0:T(4,128)(2,1)} %get-tuple-element.314), calls=%async_computation.1 | async-start | bytes 2097152 | tf_op jit(solution)/shard_map/all_to_all | solution.py:150
  141.0 1.0 copy-start.4
  142.0 40.1 %all-to-all-start.5 = ((bf16[32,2,8192]{2,1,0:T(2,128)(2,1)}), bf16[32,2,8192]{2,1,0:T(2,128)(2,1)S(1)}, u32[]{:S(2)}, u32[]{:S(2)}) async-start(bf16[32,2,8192]{2,1,0:T(2,128)(2,1)} %reshape.258), calls=%async_computation.5 | async-start | bytes 2097152 | tf_op jit(solution)/shard_map/all_to_all | solution.py:192
  154.4 6.0 copy-start.5
  182.1 37.0 %all-to-all-start.4 = ((bf16[32,2,8192]{2,1,0:T(2,128)(2,1)}), bf16[32,2,8192]{2,1,0:T(2,128)(2,1)S(1)}, u32[]{:S(2)}, u32[]{:S(2)}) async-start(bf16[32,2,8192]{2,1,0:T(2,128)(2,1)} %reshape.256), calls=%async_computation.4 | async-start | bytes 2097152 | tf_op jit(solution)/shard_map/all_to_all | solution.py:190
  219.1 42.1 %all-to-all-start.7 = ((bf16[32,2,8192]{2,1,0:T(2,128)(2,1)}), bf16[32,2,8192]{2,1,0:T(2,128)(2,1)S(1)}, u32[]{:S(2)}, u32[]{:S(2)}) async-start(bf16[32,2,8192]{2,1,0:T(2,128)(2,1)} %reshape.260), calls=%async_computation.7 | async-start | bytes 2097152 | tf_op jit(solution)/shard_map/all_to_all | solution.py:191
  236.4 0.8 copy-start.6
  253.5 17.4 %copy-start.8 = (s32[1,4096]{1,0:T(1,128)S(1)}, s32[1,4096]{1,0:T(1,128)}, u32[]{:S(2)}) copy-start(s32[1,4096]{1,0:T(1,128)} %param.27) | copy-start | bytes 49156
  261.1 42.9 %all-to-all-start.2 = ((bf16[32,2,8192]{2,1,0:T(2,128)(2,1)}), bf16[32,2,8192]{2,1,0:T(2,128)(2,1)}, u32[]{:S(2)}, u32[]{:S(2)}) async-start(bf16[32,2,8192]{2,1,0:T(2,128)(2,1)} %reshape.254), calls=%async_computation.2 | async-start | bytes 2097152 | tf_op jit(solution)/shard_map/all_to_all | solution.py:189
  270.5 455.1 %reduce-scatter.7.cloned.1.call-start = ((), (), s32[]{:S(2)}) async-start(), calls=%async_computation.12 | async-start | bytes 1351680
  477.1 34.1 %copy-start.7 = (bf16[32,4,2560]{2,1,0:T(4,128)(2,1)S(1)}, bf16[32,4,2560]{2,1,0:T(4,128)(2,1)}, u32[]{:S(2)}) copy-start(bf16[32,4,2560]{2,1,0:T(4,128)(2,1)} %copy-done.6) | copy-start | bytes 1966084
  477.1 34.1 %copy-start.9 = (bf16[64,4096]{1,0:T(8,128)(2,1)S(1)}, bf16[64,4096]{1,0:T(8,128)(2,1)}, u32[]{:S(2)}) copy-start(bf16[64,4096]{1,0:T(8,128)(2,1)} %param.25) | copy-start | bytes 1572868
  511.2 487.6 %copy-start.1 = (bf16[1,32,4,4096]{3,2,1,0:T(4,128)(2,1)S(1)}, bf16[1,32,4,4096]{3,2,1,0:T(4,128)(2,1)}, u32[]{:S(2)}) copy-start(bf16[1,32,4,4096]{3,2,1,0:T(4,128)(2,1)} %param.21) | copy-start | bytes 3145732
  513.3 434.6 %reduce-scatter.5.cloned.1.call-start = ((), (), s32[]{:S(2)}) async-start(), calls=%async_computation.11 | async-start | bytes 1081344 | tf_op jit(solution)/shard_map/reduce_scatter | solution.py:229
Sparse Core Ops, SparseCore 0:
  513.5 212.1 reduce-scatter.6
  730.0 217.8 reduce-scatter.4
where the time goes:
time: 1020 us; the launch traced here: 1010 us
  waiting for transfers between devices  463 us (45%)
  local copies, waits for them, and re-layouts  164 us (16%)
  blocking collectives  146 us (14%)
  matrix products  66.3 us (6%)
  loops' own time  57.6 us (6%)
  starting transfers between devices  50.3 us (5%)
  other arithmetic  44.8 us (4%)
  between operations  14.8 us (1%)
    reduce_scatter x1, waiting for transfers between devices, per_device(): lax.psum_scatter(up_part, 'seq', scatter_dimension=1, tiled=True)  221 us
    unnamed x3, waiting for transfers between devices  210 us
    unnamed x31, local copies, waits for them, and re-layouts  63.7 us
    psum x1, blocking collectives, per_device(): down_total, up_total = lax.psum((down_share, up_share), 'dp')  49.7 us
    another operation x1, loops' own time, attend_head(): lax.map(piece_pass, jnp.arange(total_pieces, dtype=jnp.int32))  41.9 us
    all_to_all x1, blocking collectives, per_device(): lax.all_to_all(dquery_head.reshape(block_count, length // block_count, he...  33.4 us
    all_to_all x1, blocking collectives, per_device(): lax.all_to_all(pack_blocks(keys_local, send_index, send_valid), 'dp', spl...  31.6 us
    all_to_all x1, blocking collectives, per_device(): lax.all_to_all(pack_blocks(values_local, send_index, send_valid), 'dp', s...  31.3 us
  transfers between devices with their start and end apart: 8, of which 5 were waited for; matrix products, arithmetic and copies ran while one was open for 14% of the time, Pallas kernels for 0%

commit v1 on v0

v1 whole, which is shorter than its diff:
```python
import functools
import math

import jax
import jax.numpy as jnp
from jax import lax
from jax.experimental import pallas as pl
from jax.experimental.pallas import tpu as pltpu
from jax.sharding import PartitionSpec as P

CAP = 2
HEAD = 128
RANK = 64
TOKENS = 4
LIVE = 20
ROWS = LIVE * TOKENS
FOLD = 48
MESH = pl.DeviceIdType.MESH
BF16 = jnp.bfloat16
F32 = jnp.float32
VMEM_LIMIT = 56 * 1024 * 1024


def block_tables(plan, group, groups):
    blocks = plan.shape[1]
    live_plan = plan[:, :LIVE]
    source = live_plan // blocks
    local = live_plan % blocks
    shift = jnp.arange(1, groups, dtype=jnp.int32)
    slot = jnp.arange(CAP, dtype=jnp.int32)
    place = jnp.arange(LIVE, dtype=jnp.int32)
    before = place[None, :] < place[:, None]

    dest = (group + shift) % groups
    dest_source = jnp.take(source, dest, axis=0)
    dest_local = jnp.take(local, dest, axis=0)
    match = dest_source == group
    rank = jnp.sum((before[None] & match[:, None, :]).astype(jnp.int32), axis=2)
    chosen = match[:, :, None] & (rank[:, :, None] == slot)
    send = jnp.sum(jnp.where(chosen, dest_local[:, :, None], 0), axis=1).reshape(-1)

    own_source = lax.dynamic_index_in_dim(source, group, 0, keepdims=False)
    own_local = lax.dynamic_index_in_dim(local, group, 0, keepdims=False)
    stays = own_source == group
    own_shift = (group - own_source + groups) % groups
    own_rank = jnp.sum((before & (own_source[None, :] == own_source[:, None])).astype(jnp.int32), axis=1)
    take = jnp.where(stays, 0, (own_shift - 1) * CAP + own_rank)
    hit = (own_shift[None, None, :] == shift[:, None, None]) & (own_rank[None, None, :] == slot[None, :, None])
    back = (LIVE + jnp.sum(jnp.where(hit, place - LIVE, 0), axis=2)).reshape(-1)
    home = jnp.where(stays, own_local, 0)
    return jnp.concatenate([send, take, back, home, stays.astype(jnp.int32)])


def exchange_kernel(
    groups, heads, tab, keys_in, values_in, base_in, grad_in, feat_in, down_ref, up_ref,
    keys_out, values_out, query_out, grad_out, adapter_out, feat_out,
    keys_pool, values_pool, query_pool, adapter_pool,
    keys_here, values_here, query_here, adapter_here, grad_buf, feat_buf,
    keys_send, values_send, query_send, adapter_send,
    keys_stage, values_stage, query_stage, grad_stage, adapter_stage, rows32, feat32, up32, adapter32,
    load_sem, own_sem, z_send, z_recv, s_send, s_recv,
):
    me_dp = lax.axis_index("dp")
    me_seq = lax.axis_index("seq")
    slots = (groups - 1) * CAP
    blocks = keys_in.shape[0]
    take_at = slots
    home_at = slots + LIVE + slots
    stay_at = home_at + LIVE

    loads = [
        pltpu.make_async_copy(keys_in, keys_here, load_sem.at[0]),
        pltpu.make_async_copy(values_in, values_here, load_sem.at[1]),
        pltpu.make_async_copy(grad_in, grad_buf, load_sem.at[2]),
        pltpu.make_async_copy(feat_in, feat_buf, load_sem.at[3]),
        pltpu.make_async_copy(base_in, query_here, load_sem.at[4]),
    ]
    for copy in loads:
        copy.start()

    barrier = pltpu.get_barrier_semaphore()

    def greet_dp(k, carry):
        pl.semaphore_signal(
            barrier, inc=1, device_id=(lax.rem(me_dp + k, groups), me_seq), device_id_type=MESH
        )
        return carry

    def greet_seq(k, carry):
        pl.semaphore_signal(
            barrier, inc=1, device_id=(me_dp, lax.rem(me_seq + k, heads)), device_id_type=MESH
        )
        return carry

    lax.fori_loop(1, groups, greet_dp, 0)
    lax.fori_loop(1, heads, greet_seq, 0)

    def pack(here, send):
        for i in range(slots):
            send[i] = here[tab[i]]

    def send_dp(send, pool, index):
        def one(k, carry):
            pltpu.make_async_remote_copy(
                src_ref=send.at[pl.ds((k - 1) * CAP, CAP)],
                dst_ref=pool.at[pl.ds((k - 1) * CAP, CAP)],
                send_sem=z_send.at[index],
                recv_sem=z_recv.at[index],
                device_id=(lax.rem(me_dp + k, groups), me_seq),
                device_id_type=MESH,
            ).start()
            return carry

        lax.fori_loop(1, groups, one, 0)

    def dp_total(send, pool, index):
        return pltpu.make_async_remote_copy(
            src_ref=send,
            dst_ref=pool,
            send_sem=z_send.at[index],
            recv_sem=z_recv.at[index],
            device_id=(lax.rem(me_dp + 1, groups), me_seq),
            device_id_type=MESH,
        )

    def send_seq(stage, out, index, same):
        def one(k, carry):
            peer = lax.rem(me_seq + k, heads)
            pltpu.make_async_remote_copy(
                src_ref=stage.at[0] if same else stage.at[peer],
                dst_ref=out.at[k],
                send_sem=s_send.at[index],
                recv_sem=s_recv.at[index],
                device_id=(me_dp, peer),
                device_id_type=MESH,
            ).start()
            return carry

        lax.fori_loop(1, heads, one, 0)
        pltpu.make_async_copy(
            stage.at[0] if same else stage.at[me_seq], out.at[0], own_sem.at[index]
        ).start()

    def seq_total(out, index):
        return pltpu.make_async_remote_copy(
            src_ref=out.at[pl.ds(1, heads - 1)],
            dst_ref=out.at[pl.ds(1, heads - 1)],
            send_sem=s_send.at[index],
            recv_sem=s_recv.at[index],
            device_id=(me_dp, lax.rem(me_seq + 1, heads)),
            device_id_type=MESH,
        )

    def to_heads(stage):
        for h in range(heads):
            stage[h] = rows32[:, h * HEAD:(h + 1) * HEAD].astype(BF16)

    def dest_block(pool, here, j):
        moved = pool[tab[take_at + j]].astype(F32)
        kept = here[tab[home_at + j]].astype(F32)
        return jnp.where(tab[stay_at + j] == 1, kept, moved)

    def unpack(pool, here, stage):
        for j in range(LIVE):
            rows32[j * TOKENS:(j + 1) * TOKENS, :] = dest_block(pool, here, j)
        to_heads(stage)

    loads[0].wait()
    pack(keys_here, keys_send)
    pl.semaphore_wait(barrier, groups + heads - 2)
    send_dp(keys_send, keys_pool, 0)
    loads[1].wait()
    pack(values_here, values_send)
    send_dp(values_send, values_pool, 1)

    loads[2].wait()
    for j in range(LIVE):
        rows32[j * TOKENS:(j + 1) * TOKENS, :] = grad_buf[j].astype(F32)
    to_heads(grad_stage)
    send_seq(grad_stage, grad_out, 3, False)

    loads[3].wait()
    loads[4].wait()
    for b in range(blocks):
        feat32[b * TOKENS:(b + 1) * TOKENS, :] = feat_buf[b].astype(F32)
    nt = (((1,), (1,)), ((), ()))
    features = feat32[: blocks * TOKENS, :].astype(BF16)
    adapter = lax.dot_general(features, down_ref[...], nt, preferred_element_type=F32).astype(BF16)
    doubled = jnp.concatenate([adapter, adapter], axis=1).astype(F32)
    adapter32[: blocks * TOKENS, :] = doubled
    up32[...] = jnp.dot(adapter, up_ref[...], preferred_element_type=F32)
    for b in range(blocks):
        query_here[b] = (
            query_here[b].astype(F32) + up32[b * TOKENS:(b + 1) * TOKENS, :]
        ).astype(BF16)
        adapter_here[b] = adapter32[b * TOKENS:(b + 1) * TOKENS, :].astype(BF16)
    pack(query_here, query_send)
    send_dp(query_send, query_pool, 2)
    pack(adapter_here, adapter_send)
    send_dp(adapter_send, adapter_pool, 3)

    for i in range(slots):
        feat32[i * TOKENS:(i + 1) * TOKENS, :] = feat_buf[tab[i]].astype(F32)
    for j in range(LIVE):
        feat32[(slots + j) * TOKENS:(slots + j + 1) * TOKENS, :] = feat_buf[tab[home_at + j]].astype(F32)
    feat_out[...] = feat32[: (slots + LIVE) * TOKENS, :].astype(BF16)

    dp_total(keys_send, keys_pool, 0).wait_recv()
    unpack(keys_pool, keys_here, keys_stage)
    send_seq(keys_stage, keys_out, 0, False)
    dp_total(values_send, values_pool, 1).wait_recv()
    unpack(values_pool, values_here, values_stage)
    send_seq(values_stage, values_out, 1, False)
    dp_total(query_send, query_pool, 2).wait_recv()
    unpack(query_pool, query_here, query_stage)
    send_seq(query_stage, query_out, 2, False)
    dp_total(adapter_send, adapter_pool, 3).wait_recv()
    adapter32[...] = jnp.zeros_like(adapter32)
    for j in range(LIVE):
        adapter32[j * TOKENS:(j + 1) * TOKENS, :] = dest_block(adapter_pool, adapter_here, j)
    lane = lax.broadcasted_iota(jnp.int32, (FOLD, HEAD), 1)
    adapter_stage[0] = jnp.where(
        lane < RANK, adapter32[0:FOLD, :], adapter32[FOLD:2 * FOLD, :]
    ).astype(BF16)
    send_seq(adapter_stage, adapter_out, 4, True)

    dp_total(keys_send, keys_pool, 0).wait_send()
    dp_total(values_send, values_pool, 1).wait_send()
    dp_total(query_send, query_pool, 2).wait_send()
    dp_total(adapter_send, adapter_pool, 3).wait_send()
    outs = (keys_out, values_out, query_out, grad_out, adapter_out)
    stages = (keys_stage, values_stage, query_stage, grad_stage, adapter_stage)
    for index in (3, 0, 1, 2, 4):
        own = stages[index].at[0]
        pltpu.make_async_copy(own, outs[index].at[0], own_sem.at[index]).wait()
        seq_total(outs[index], index).wait_recv()
        seq_total(outs[index], index).wait_send()


def exchange(tables, keys, values, base, grads, features, down_t, up, groups, heads):
    blocks = keys.shape[0]
    slots = (groups - 1) * CAP
    width = heads * HEAD
    inputs = features.shape[2]
    vmem = pl.BlockSpec(memory_space=pltpu.VMEM)
    hbm = pl.BlockSpec(memory_space=pl.ANY)
    chunk = jax.ShapeDtypeStruct((heads, ROWS, HEAD), BF16)
    feat_rows = (slots + LIVE) * TOKENS
    adapter_rows = max(blocks * TOKENS, 2 * FOLD)
    return pl.pallas_call(
        functools.partial(exchange_kernel, groups, heads),
        out_shape=(
            chunk, chunk, chunk, chunk,
            jax.ShapeDtypeStruct((heads, FOLD, HEAD), BF16),
            jax.ShapeDtypeStruct((feat_rows, inputs), BF16),
        ),
        in_specs=[pl.BlockSpec(memory_space=pltpu.SMEM)] + [hbm] * 5 + [vmem] * 2,
        out_specs=[hbm] * 5 + [vmem],
        scratch_shapes=[
            pltpu.VMEM((slots, TOKENS, width), BF16),
            pltpu.VMEM((slots, TOKENS, width), BF16),
            pltpu.VMEM((slots, TOKENS, width), BF16),
            pltpu.VMEM((slots, TOKENS, HEAD), BF16),
            pltpu.VMEM((blocks, TOKENS, width), BF16),
            pltpu.VMEM((blocks, TOKENS, width), BF16),
            pltpu.VMEM((blocks, TOKENS, width), BF16),
            pltpu.VMEM((blocks, TOKENS, HEAD), BF16),
            pltpu.VMEM((blocks, TOKENS, width), BF16),
            pltpu.VMEM((blocks, TOKENS, inputs), BF16),
            pltpu.VMEM((slots, TOKENS, width), BF16),
            pltpu.VMEM((slots, TOKENS, width), BF16),
            pltpu.VMEM((slots, TOKENS, width), BF16),
            pltpu.VMEM((slots, TOKENS, HEAD), BF16),
            pltpu.VMEM((heads, ROWS, HEAD), BF16),
            pltpu.VMEM((heads, ROWS, HEAD), BF16),
            pltpu.VMEM((heads, ROWS, HEAD), BF16),
            pltpu.VMEM((heads, ROWS, HEAD), BF16),
            pltpu.VMEM((1, FOLD, HEAD), BF16),
            pltpu.VMEM((ROWS, width), F32),
            pltpu.VMEM((max(feat_rows, blocks * TOKENS), inputs), F32),
            pltpu.VMEM((blocks * TOKENS, width), F32),
            pltpu.VMEM((adapter_rows, HEAD), F32),
            pltpu.SemaphoreType.DMA((5,)),
            pltpu.SemaphoreType.DMA((5,)),
            pltpu.SemaphoreType.DMA((4,)),
            pltpu.SemaphoreType.DMA((4,)),
            pltpu.SemaphoreType.DMA((5,)),
            pltpu.SemaphoreType.DMA((5,)),
        ],
        compiler_params=pltpu.CompilerParams(
            collective_id=1, has_side_effects=True, vmem_limit_bytes=VMEM_LIMIT
        ),
        name="exchange",
    )(tables, keys, values, base, grads, features, down_t, up)


def attention_kernel(
    heads, tile, info, query_ref, key_ref, value_ref, grad_ref, adapter_ref, up_ref,
    partial_ref, up_grad_ref, log_ref,
    key_max, key_sum, value_sum, value_neg, scores, probs, dquery, logs,
):
    total = heads * ROWS
    me_seq = info[0]
    live_count = info[1]
    scaling = 1.0 / math.sqrt(HEAD)
    to_exp2 = scaling * math.log2(math.e)
    nt = (((1,), (1,)), ((), ()))
    tn = (((0,), (0,)), ((), ()))

    def position(first, rows):
        token = first + lax.broadcasted_iota(jnp.int32, (rows, HEAD), 0)
        part = (token * 52429) >> 22
        rest = token - part * ROWS
        owner = (me_seq - part) & (heads - 1)
        return (rest >> 2) * (TOKENS * heads) + owner * TOKENS + (rest & 3)

    first_row = pl.multiple_of(me_seq * ROWS, 16)
    filler = key_ref[pl.ds(first_row, 16), :][0:1, :]
    lane = lax.broadcasted_iota(jnp.int32, (ROWS, HEAD), 1)
    for k in range(heads):
        at = slice(k * ROWS, (k + 1) * ROWS)
        live = position(k * ROWS, ROWS) < live_count
        rows = key_ref[at, :]
        zero = jnp.zeros((), BF16)
        value = jnp.where(live, value_ref[at, :], zero)
        key_max[at, :] = jnp.where(live, rows, filler)
        key_sum[at, :] = jnp.where(live, rows, zero)
        value_sum[at, 0:HEAD] = value
        value_sum[at, HEAD:] = jnp.where(live, 1.0, 0.0).astype(BF16)
        value_neg[at, 0:HEAD] = value
        value_neg[at, HEAD:] = jnp.where(lane < 3, -1.0, 0.0).astype(BF16)

    lanes = lax.broadcasted_iota(jnp.int32, (tile, HEAD), 1)

    def one_tile(index, carry):
        first = pl.multiple_of(index * tile, tile)
        query = query_ref[pl.ds(first, tile), :]
        grad = grad_ref[pl.ds(first, tile), :]
        scores[...] = lax.dot_general(query, key_max[...], nt, preferred_element_type=F32)
        maximum = jnp.max(scores[...], axis=1, keepdims=True)
        probs[...] = jnp.exp2((scores[...] - maximum) * to_exp2).astype(BF16)
        summed = jnp.dot(probs[...], value_sum[...], preferred_element_type=F32)
        norm = summed[:, HEAD:]
        inverse = 1.0 / norm
        delta = jnp.sum(grad.astype(F32) * summed[:, :HEAD], axis=1, keepdims=True) * inverse
        high = delta.astype(BF16)
        middle = (delta - high.astype(F32)).astype(BF16)
        low = (delta - high.astype(F32) - middle.astype(F32)).astype(BF16)
        zero = jnp.zeros((), BF16)
        parts = jnp.where(lanes == 0, high, jnp.where(lanes == 1, middle, jnp.where(lanes == 2, low, zero)))
        wide = jnp.concatenate([grad, parts], axis=1)
        dprob = lax.dot_general(wide, value_neg[...], nt, preferred_element_type=F32)
        dscore = (probs[...].astype(F32) * dprob).astype(BF16)
        result = jnp.dot(dscore, key_sum[...], preferred_element_type=F32) * (inverse * scaling)
        live = position(first, tile) < live_count
        dquery[pl.ds(first, tile), :] = jnp.where(live, result, 0.0).astype(BF16)
        logs[pl.ds(first, tile), :] = jnp.where(live, maximum * scaling + jnp.log(norm), 0.0)
        return carry

    lax.fori_loop(0, total // tile, one_tile, 0)

    blank = jnp.zeros((ROWS, HEAD), F32)
    gathered = blank
    row = lax.broadcasted_iota(jnp.int32, (ROWS, HEAD), 0)
    for k in range(heads):
        owner = (me_seq - k) & (heads - 1)
        column = owner * TOKENS + (row & 3)
        gathered = gathered + jnp.where(lane == column, logs[k * ROWS:(k + 1) * ROWS, :], blank)
    pick = lax.broadcasted_iota(jnp.int32, (24, ROWS), 1) >> 2
    pick = (pick == lax.broadcasted_iota(jnp.int32, (24, ROWS), 0)).astype(F32)
    log_ref[...] = jnp.dot(pick, gathered, preferred_element_type=F32, precision=lax.Precision.HIGHEST)

    up = up_ref[...]
    nothing = jnp.zeros((RANK, HEAD), BF16)
    to_low = jnp.concatenate([up, nothing], axis=0)
    to_high = jnp.concatenate([nothing, up], axis=0)
    up_total = jnp.zeros((RANK, HEAD), F32)
    for k in range(heads):
        first_part = dquery[k * ROWS:k * ROWS + FOLD, :]
        second_part = jnp.concatenate(
            [dquery[k * ROWS + FOLD:(k + 1) * ROWS, :], jnp.zeros((2 * FOLD - ROWS, HEAD), BF16)], axis=0
        )
        partial_ref[k] = (
            lax.dot_general(first_part, to_low, nt, preferred_element_type=F32)
            + lax.dot_general(second_part, to_high, nt, preferred_element_type=F32)
        ).astype(BF16)
        folded = adapter_ref[k]
        up_total = up_total + lax.dot_general(folded, first_part, tn, preferred_element_type=F32)[:RANK]
        up_total = up_total + lax.dot_general(folded, second_part, tn, preferred_element_type=F32)[RANK:]
    up_grad_ref[...] = up_total


def attention(info, query, keys, values, grads, adapter, up, heads):
    total = heads * ROWS
    tile = 256 if total % 256 == 0 else ROWS
    vmem = pl.BlockSpec(memory_space=pltpu.VMEM)
    return pl.pallas_call(
        functools.partial(attention_kernel, heads, tile),
        out_shape=(
            jax.ShapeDtypeStruct((heads, FOLD, HEAD), BF16),
            jax.ShapeDtypeStruct((RANK, HEAD), F32),
            jax.ShapeDtypeStruct((24, HEAD), F32),
        ),
        in_specs=[pl.BlockSpec(memory_space=pltpu.SMEM)] + [vmem] * 6,
        out_specs=[vmem] * 3,
        scratch_shapes=[
            pltpu.VMEM((total, HEAD), BF16),
            pltpu.VMEM((total, HEAD), BF16),
            pltpu.VMEM((total, 2 * HEAD), BF16),
            pltpu.VMEM((total, 2 * HEAD), BF16),
            pltpu.VMEM((tile, total), F32),
            pltpu.VMEM((tile, total), BF16),
            pltpu.VMEM((total, HEAD), BF16),
            pltpu.VMEM((total, HEAD), F32),
        ],
        compiler_params=pltpu.CompilerParams(vmem_limit_bytes=VMEM_LIMIT),
        name="attention",
    )(info, query, keys, values, grads, adapter, up)


def reduce_kernel(
    groups, heads, scale, tab, partial_ref, up_ref, feat_ref,
    down_out, up_out,
    partial_recv, blocks32, pieces, grads_send, grads_recv, down_send, down_recv,
    share_send, share_recv, up_recv,
    s_send, s_recv, z_send, z_recv,
):
    me_dp = lax.axis_index("dp")
    me_seq = lax.axis_index("seq")
    slots = (groups - 1) * CAP
    back_at = slots + LIVE
    stay_at = back_at + slots + LIVE
    tn = (((0,), (0,)), ((), ()))

    barrier = pltpu.get_barrier_semaphore()

    def greet_dp(k, carry):
        pl.semaphore_signal(
            barrier, inc=1, device_id=(lax.rem(me_dp + k, groups), me_seq), device_id_type=MESH
        )
        return carry

    def greet_seq(k, carry):
        pl.semaphore_signal(
            barrier, inc=1, device_id=(me_dp, lax.rem(me_seq + k, heads)), device_id_type=MESH
        )
        return carry

    lax.fori_loop(1, groups, greet_dp, 0)
    lax.fori_loop(1, heads, greet_seq, 0)
    pl.semaphore_wait(barrier, groups + heads - 2)

    def seq_copy(k, src, dst, index):
        return pltpu.make_async_remote_copy(
            src_ref=src, dst_ref=dst, send_sem=s_send.at[index], recv_sem=s_recv.at[index],
            device_id=(me_dp, k), device_id_type=MESH,
        )

    def dp_copy(k, src, dst, index):
        return pltpu.make_async_remote_copy(
            src_ref=src, dst_ref=dst, send_sem=z_send.at[index], recv_sem=z_recv.at[index],
            device_id=(k, me_seq), device_id_type=MESH,
        )

    def send_partial(k, carry):
        seq_copy(lax.rem(me_seq + heads - k, heads), partial_ref.at[k], partial_recv.at[k - 1], 0).start()
        return carry

    lax.fori_loop(1, heads, send_partial, 0)

    def send_up(k, carry):
        dp_copy(lax.rem(me_dp + k, groups), up_ref, up_recv.at[k - 1], 0).start()
        return carry

    lax.fori_loop(1, groups, send_up, 0)

    partial_total = seq_copy(lax.rem(me_seq + 1, heads), partial_ref.at[pl.ds(1, heads - 1)], partial_recv, 0)
    partial_total.wait_recv()
    folded = partial_ref[0].astype(F32)
    for k in range(heads - 1):
        folded = folded + partial_recv[k].astype(F32)
    turned = pltpu.roll(folded, RANK, 1)
    for j in range(LIVE):
        row = j * TOKENS
        from_ref = folded if row < FOLD else turned
        row = row if row < FOLD else row - FOLD
        blocks32[j] = from_ref[row:row + TOKENS, :]
    blocks32[LIVE] = jnp.zeros((TOKENS, HEAD), F32)

    for i in range(slots):
        k, slot = i // CAP, i % CAP
        grads_send[k, slot * TOKENS:(slot + 1) * TOKENS, :] = blocks32[tab[back_at + i]]

    def send_grads(k, carry):
        dp_copy(lax.rem(me_dp + groups - k, groups), grads_send.at[k - 1], grads_recv.at[k - 1], 1).start()
        return carry

    lax.fori_loop(1, groups, send_grads, 0)
    for j in range(LIVE):
        stays = (tab[stay_at + j]).astype(F32)
        pieces[slots * TOKENS + j * TOKENS:slots * TOKENS + (j + 1) * TOKENS, :] = blocks32[j] * stays
    grads_total = dp_copy(lax.rem(me_dp + 1, groups), grads_send, grads_recv, 1)
    grads_total.wait_recv()
    for k in range(groups - 1):
        pieces[k * 2 * TOKENS:(k + 1) * 2 * TOKENS, :] = grads_recv[k]

    adapter_grad = pieces[...].astype(BF16)[:, :RANK]
    doubled = jnp.concatenate([adapter_grad, adapter_grad], axis=1)
    lane = lax.broadcasted_iota(jnp.int32, (FOLD, HEAD), 1)
    transposed = lax.dot_general(doubled, feat_ref[...], tn, preferred_element_type=F32)
    down = transposed.T
    for h in range(heads):
        first = down[h * ROWS:h * ROWS + FOLD, :]
        second = jnp.concatenate(
            [down[h * ROWS + FOLD:(h + 1) * ROWS, :], jnp.zeros((2 * FOLD - ROWS, HEAD), F32)], axis=0
        )
        down_send[h] = jnp.where(lane < RANK, first, second).astype(BF16)

    def send_down(k, carry):
        peer = lax.rem(me_seq + k, heads)
        seq_copy(peer, down_send.at[peer], down_recv.at[k - 1], 1).start()
        return carry

    lax.fori_loop(1, heads, send_down, 0)
    down_total = seq_copy(lax.rem(me_seq + 1, heads), down_send.at[pl.ds(0, heads - 1)], down_recv, 1)
    down_total.wait_recv()
    share = down_send[me_seq].astype(F32)
    for k in range(heads - 1):
        share = share + down_recv[k].astype(F32)
    share_send[...] = share

    def send_share(k, carry):
        dp_copy(lax.rem(me_dp + k, groups), share_send, share_recv.at[k - 1], 2).start()
        return carry

    lax.fori_loop(1, groups, send_share, 0)
    up_total = dp_copy(lax.rem(me_dp + 1, groups), up_recv, up_recv, 0)
    up_total.wait_recv()
    up_sum = up_ref[...]
    for k in range(groups - 1):
        up_sum = up_sum + up_recv[k]
    up_out[...] = up_sum * scale
    share_total = dp_copy(lax.rem(me_dp + 1, groups), share_recv, share_recv, 2)
    share_total.wait_recv()
    for k in range(groups - 1):
        share = share + share_recv[k]
    share = share * scale
    turned = pltpu.roll(share, RANK, 1)
    whole = jnp.concatenate(
        [share, turned[:ROWS - FOLD], jnp.zeros((HEAD - ROWS, HEAD), F32)], axis=0
    )
    down_out[...] = whole.T[:RANK, :ROWS]

    partial_total.wait_send()
    up_total.wait_send()
    grads_total.wait_send()
    down_total.wait_send()
    share_total.wait_send()


def reduce_gradients(tables, partial, up_part, feat_rows, scale, groups, heads):
    slots = (groups - 1) * CAP
    vmem = pl.BlockSpec(memory_space=pltpu.VMEM)
    return pl.pallas_call(
        functools.partial(reduce_kernel, groups, heads, scale),
        out_shape=(
            jax.ShapeDtypeStruct((RANK, ROWS), F32),
            jax.ShapeDtypeStruct((RANK, HEAD), F32),
        ),
        in_specs=[pl.BlockSpec(memory_space=pltpu.SMEM)] + [vmem] * 3,
        out_specs=[vmem] * 2,
        scratch_shapes=[
            pltpu.VMEM((heads - 1, FOLD, HEAD), BF16),
            pltpu.VMEM((LIVE + 1, TOKENS, HEAD), F32),
            pltpu.VMEM(((slots + LIVE) * TOKENS, HEAD), F32),
            pltpu.VMEM((groups - 1, CAP * TOKENS, HEAD), F32),
            pltpu.VMEM((groups - 1, CAP * TOKENS, HEAD), F32),
            pltpu.VMEM((heads, FOLD, HEAD), BF16),
            pltpu.VMEM((heads - 1, FOLD, HEAD), BF16),
            pltpu.VMEM((FOLD, HEAD), F32),
            pltpu.VMEM((groups - 1, FOLD, HEAD), F32),
            pltpu.VMEM((groups - 1, RANK, HEAD), F32),
            pltpu.SemaphoreType.DMA((2,)),
            pltpu.SemaphoreType.DMA((2,)),
            pltpu.SemaphoreType.DMA((3,)),
            pltpu.SemaphoreType.DMA((3,)),
        ],
        compiler_params=pltpu.CompilerParams(
            collective_id=2, has_side_effects=True, vmem_limit_bytes=VMEM_LIMIT
        ),
        name="reduce_gradients",
    )(tables, partial, up_part, feat_rows)


def per_device(
    features, frozen_query_weight, source_keys, source_values, output_gradient,
    adapter_down_weight, adapter_up_weight, source_block_plan, segments,
):
    groups = lax.axis_size("dp")
    heads = lax.axis_size("seq")
    group = lax.axis_index("dp")
    head = lax.axis_index("seq")
    tables = block_tables(source_block_plan, group, groups)
    live_count = jnp.sum((segments[0] < 1).astype(jnp.int32))
    info = jnp.stack([head.astype(jnp.int32), live_count])
    keys, values, query, grads, adapter, feat_rows = exchange(
        tables, source_keys[0], source_values[0], frozen_query_weight[0], output_gradient[0], features[0],
        adapter_down_weight.T, adapter_up_weight, groups, heads,
    )
    total = heads * ROWS
    up_head = lax.dynamic_slice_in_dim(adapter_up_weight, head * HEAD, HEAD, 1)
    partial, up_part, logs = attention(
        info, query.reshape(total, HEAD), keys.reshape(total, HEAD), values.reshape(total, HEAD),
        grads.reshape(total, HEAD), adapter, up_head, heads,
    )
    length = segments.shape[1]
    scale = 4.0 / math.sqrt(groups * length)
    down, up = reduce_gradients(tables, partial, up_part, feat_rows, scale, groups, heads)
    log_norm = logs[:LIVE, : TOKENS * heads].reshape(-1)
    log_norm = jnp.pad(log_norm, (0, length - log_norm.shape[0]))
    return (down.T, up, log_norm[None, None])


def solution(mesh):
    in_specs = (
        P("dp", None, "seq", None),
        P("dp", None, "seq", None),
        P("dp", None, "seq", None),
        P("dp", None, "seq", None),
        P("dp", None, "seq", None),
        P(),
        P(),
        P(),
        P("dp", None),
    )
    out_specs = (P("seq", None), P(None, "seq"), P("dp", "seq", None))
    return jax.shard_map(
        per_device, mesh=mesh, in_specs=in_specs, out_specs=out_specs, check_vma=False
    )
```

time: 1020 us -> 206 us (0.20); the launches traced: 1010 us -> 204 us
  waiting for transfers between devices: 463 us -> 0 us
  Pallas kernels: 0 us -> 193 us
  local copies, waits for them, and re-layouts: 164 us -> 6.72 us
  blocking collectives: 146 us -> 0 us
  matrix products: 66.3 us -> 0 us
  loops' own time: 57.6 us -> 0 us
  starting transfers between devices: 50.3 us -> 0 us
  other arithmetic: 44.8 us -> 3.54 us
  between operations: 14.8 us -> 0.77 us
    reduce_scatter x1 -> x0, waiting for transfers between devices: 221 us -> none  [per_device(): lax.psum_scatter(up_part, 'seq', scatter_dimension=1, tiled=True)]
    unnamed x3 -> x0, waiting for transfers between devices: 210 us -> none
    pallas_call x0 -> x3, Pallas kernels: none -> 193 us  [the longest x1 114 us: exchange(): pl.pallas_call(functools.partial(exchange_kernel, groups, heads), out_sha...]
    all_to_all x3 -> x0, blocking collectives: 96.3 us -> none  [the longest x1 33.4 us: per_device(): lax.all_to_all(dquery_head.reshape(block_count, length // block_count, he...]
    dot_general x28 -> x0, matrix products: 66.3 us -> none  [the longest x8 24.9 us: piece_pass(): jnp.dot(dscore, key_tile, preferred_element_type=jnp.float32) * scaling]
    unnamed x31 -> x12, local copies, waits for them, and re-layouts: 63.7 us -> 2.83 us
    another operation x2 -> x0, loops' own time: 57.6 us -> none  [the longest x1 41.9 us: attend_head(): lax.map(piece_pass, jnp.arange(total_pieces, dtype=jnp.int32))]
    all_to_all x6 -> x0, starting transfers between devices: 50 us -> none  [the longest x1 11.8 us: per_device(): lax.all_to_all(pack_blocks(feat_local, send_index, send_valid), 'dp', spl...]
  transfers between devices with their start and end apart: 8 -> 0, of which waited for: 5 -> 0; matrix products, arithmetic and copies ran while one was open for 14% -> 0% of each run, Pallas kernels for 0% -> 0%
where the time goes in v1:
time: 206 us; the launch traced here: 204 us
  Pallas kernels  193 us (94%)
  local copies, waits for them, and re-layouts  6.72 us (3%)
  other arithmetic  3.54 us (2%)
    pallas_call x1, Pallas kernels, exchange(): pl.pallas_call(functools.partial(exchange_kernel, groups, heads), out_sha...  114 us
    pallas_call x1, Pallas kernels, reduce_gradients(): pl.pallas_call(functools.partial(reduce_kernel, groups, heads, scale), ou...  47.7 us
    pallas_call x1, Pallas kernels, attention(): pl.pallas_call(functools.partial(attention_kernel, heads, tile), out_shap...  30.4 us

profile of v1, /device:TPU:1, one launch (start us, length us, event | category | flops | bytes accessed | tf_op | source)
XLA Modules:
  0.0 203.6 jit_solution(7298790692024660417)
XLA Ops:
  0.6 0.7 copy-done.3
  1.3 0.7 fusion
  2.0 1.2 pad_add_fusion.info
  3.3 0.6 copy-done.2
  4.0 0.6 gather_fusion
  4.6 0.1 select_compare_fusion
  4.6 0.2 convert_reduce_fusion.1
  4.8 0.6 gather_fusion.1
  5.6 0.4 fusion.2
  5.9 0.1 add.80
  6.0 0.4 convert_reduce_fusion
  6.4 0.1 copy.12
  6.5 0.3 fusion.1
  6.9 0.1 reshape.130
  7.0 0.6 concatenate.3.tab
  7.5 1.3 constant_dynamic-slice_fusion.up_ref
  8.9 114.4 %exchange.1 = (bf16[32,80,128]{2,1,0:T(8,128)(2,1)}, bf16[32,80,128]{2,1,0:T(8,128)(2,1)}, bf16[32,80,128]{2,1,0:T(8,128)(2,1)}, bf16[32,80,128]{2,1,0:T(8,128)(...) custom-call(s32[120]{0:T(128)} %concatenate.3.tab, bf16[32,4,4096]{2,1,0:T(4,128)(2,1)} %bitcast.23, ...), custom_call_target="tpu_custom_call" | custom-call | tf_op jit(solution)/shard_map/exchange/pallas_call | solution.py:250
  123.2 30.4 %attention.1 = (bf16[32,48,128]{2,1,0:T(8,128)(2,1)}, f32[64,128]{1,0:T(8,128)}, f32[24,128]{1,0:T(8,128)}) custom-call(s32[2]{0:T(128)} %pad_add_fusion.info, bf16[2560,128]{1,0:T(8,128)(2,1)} %bitcast.30, bf16[2560,128]{1,0:T(8,128)(2,1)} %bitcast.28, bf16[2560,128]{1,0:T(8,128)(2,1)} %bitcast.29, bf16[2560,128]{1,0:T(8,128)(2,1)} %bitcast.31, ...), custom_call_target="tpu_custom_call" | custom-call | tf_op jit(solution)/shard_map/attention/pallas_call | solution.py:397
  153.7 47.7 %reduce_gradients.1 = (f32[64,80]{1,0:T(8,128)}, f32[64,128]{1,0:T(8,128)}) custom-call(s32[120]{0:T(128)} %concatenate.3.tab, bf16[32,48,128]{2,1,0:T(8,128)(2,1)} %get-tuple-element.20.partial_ref, f32[64,128]{1,0:T(8,128)} %get-tuple-element.21.up_ref, bf16[200,2560]{1,0:T(8,128)(2,1)} %get-tuple-element.22.feat_ref), custom_call_target="tpu_custom_call" | custom-call | tf_op jit(solution)/shard_map/reduce_gradients/pallas_call | solution.py:564
  201.5 0.6 pad.4
  202.1 0.1 copy-done.1
  202.2 0.6 copy.15
  202.8 0.2 copy-done
  203.0 0.6 copy.16
  (21 shorter events, 0.3 us)
Async XLA Ops:
  0.6 0.7 copy-start.3
  3.2 0.7 copy-start.2
  153.7 47.8 %copy-start.4 = (f32[24,128]{1,0:T(8,128)S(1)}, f32[24,128]{1,0:T(8,128)}, u32[]{:S(2)}) copy-start(f32[24,128]{1,0:T(8,128)} %get-tuple-element.25) | copy-start | bytes 36868
  201.4 0.8 copy-start.1
  202.2 0.8 copy-start

commit v2 on v1

v2 whole, which is shorter than its diff:
```python
import functools
import math

import jax
import jax.numpy as jnp
from jax import lax
from jax.experimental import pallas as pl
from jax.experimental.pallas import tpu as pltpu
from jax.sharding import PartitionSpec as P

CAP = 2
HEAD = 128
RANK = 64
TOKENS = 4
LIVE = 20
ROWS = LIVE * TOKENS
PARTS = 4
FOLD = 48
MESH = pl.DeviceIdType.MESH
BF16 = jnp.bfloat16
F32 = jnp.float32
VMEM_LIMIT = 56 * 1024 * 1024


def tables_kernel(groups, plan_ref, tab_ref):
    group = lax.axis_index("dp")
    blocks = plan_ref.shape[1]
    shift = blocks.bit_length() - 1
    plan = plan_ref[...]
    source, local = plan >> shift, plan & (blocks - 1)
    row = lax.broadcasted_iota(jnp.int32, (groups, blocks), 0)
    place = lax.broadcasted_iota(jnp.int32, (groups, blocks), 1)
    live = place < LIVE
    first = lax.broadcasted_iota(jnp.int32, (blocks, blocks), 0)
    second = lax.broadcasted_iota(jnp.int32, (blocks, blocks), 1)
    match = live & (source == group)
    rank = jnp.dot(match.astype(F32), (first < second).astype(F32), preferred_element_type=F32)

    def column(chosen, value):
        return jnp.sum(jnp.where(chosen, value, 0), axis=1, keepdims=True)

    send = [column(match & (rank == r), local) for r in range(CAP)]
    own = jnp.sum(jnp.where(row == group, plan, 0), axis=0, keepdims=True)
    own_source, own_local = own >> shift, own & (blocks - 1)
    down_column = jnp.sum(jnp.where(first == second, own_source, 0), axis=1, keepdims=True)
    same = (down_column == own_source) & (first < second)
    own_rank = jnp.sum(same.astype(jnp.int32), axis=0, keepdims=True)
    back = [
        LIVE + column(live & (own_source == row) & (own_rank == r), place - LIVE) for r in range(CAP)
    ]
    stays = own_source == group
    distance = (group - own_source + groups) & (groups - 1)
    take = jnp.where(stays, 0, (distance - 1) * CAP + own_rank)
    tab_ref[...] = jnp.zeros_like(tab_ref)
    for at, part in enumerate(send + back):
        tab_ref[0:groups, at:at + 1] = part
    tab_ref[groups:groups + 1, 0:blocks] = take
    tab_ref[groups + 1:groups + 2, 0:blocks] = jnp.where(stays, own_local, 0)
    tab_ref[groups + 2:groups + 3, 0:blocks] = stays.astype(jnp.int32)


def block_tables(plan, groups):
    vmem = pl.BlockSpec(memory_space=pltpu.VMEM)
    return pl.pallas_call(
        functools.partial(tables_kernel, groups),
        out_shape=jax.ShapeDtypeStruct((24, HEAD), jnp.int32),
        in_specs=[vmem],
        out_specs=vmem,
        name="tables",
    )(plan)


def greet_all(groups, heads, me_dp, me_seq):
    barrier = pltpu.get_barrier_semaphore()

    def greet_dp(k, carry):
        pl.semaphore_signal(
            barrier, inc=1, device_id=(lax.rem(me_dp + k, groups), me_seq), device_id_type=MESH
        )
        return carry

    def greet_seq(k, carry):
        pl.semaphore_signal(
            barrier, inc=1, device_id=(me_dp, lax.rem(me_seq + k, heads)), device_id_type=MESH
        )
        return carry

    lax.fori_loop(1, groups, greet_dp, 0)
    lax.fori_loop(1, heads, greet_seq, 0)
    return barrier


def exchange_kernel(
    groups, heads, parts, tab, keys_in, values_in, base_in, grad_in, feat_in, down_ref, up_ref,
    keys_out, values_out, query_out, grad_out, adapter_out, feat_moving, feat_staying,
    *scratch,
):
    keys_pool, values_pool, query_pool = (scratch[n * parts:(n + 1) * parts] for n in range(3))
    (
        adapter_pool,
        keys_here, values_here, query_here, adapter_here, grad_buf, feat_buf,
        keys_send, values_send, query_send, adapter_send,
        keys_stage, values_stage, query_stage, grad_stage, adapter_stage, rows32, feat32, up32, adapter32,
        load_sem, own_sem, z_send, z_recv, s_send, s_recv,
    ) = scratch[3 * parts:]
    me_dp = lax.axis_index("dp")
    me_seq = lax.axis_index("seq")
    slots = (groups - 1) * CAP
    blocks = keys_in.shape[0]
    per_part = heads // parts

    def head_of(part, c):
        return c * parts + ((part - c) & (parts - 1))

    def slot_source(i):
        return tab[lax.rem(me_dp + 1 + i // CAP, groups), i % CAP]

    loads = [
        pltpu.make_async_copy(keys_in, keys_here, load_sem.at[0]),
        pltpu.make_async_copy(base_in, query_here, load_sem.at[1]),
        pltpu.make_async_copy(feat_in, feat_buf, load_sem.at[2]),
        pltpu.make_async_copy(grad_in, grad_buf, load_sem.at[3]),
        pltpu.make_async_copy(values_in, values_here, load_sem.at[4]),
    ]
    for copy in loads:
        copy.start()
    barrier = greet_all(groups, heads, me_dp, me_seq)

    def pack(here, send):
        for i in range(slots):
            block = here[slot_source(i)]
            for part in range(parts):
                for c in range(per_part):
                    h = head_of(part, c)
                    send[part, i, :, c * HEAD:(c + 1) * HEAD] = block[:, h * HEAD:(h + 1) * HEAD]

    def send_dp(send, pool, index):
        def one(k, carry):
            pltpu.make_async_remote_copy(
                src_ref=send.at[pl.ds((k - 1) * CAP, CAP)],
                dst_ref=pool.at[pl.ds((k - 1) * CAP, CAP)],
                send_sem=z_send.at[index],
                recv_sem=z_recv.at[index],
                device_id=(lax.rem(me_dp + k, groups), me_seq),
                device_id_type=MESH,
            ).start()
            return carry

        lax.fori_loop(1, groups, one, 0)

    def dp_total(send, pool, index):
        return pltpu.make_async_remote_copy(
            src_ref=send,
            dst_ref=pool,
            send_sem=z_send.at[index],
            recv_sem=z_recv.at[index],
            device_id=(lax.rem(me_dp + 1, groups), me_seq),
            device_id_type=MESH,
        )

    def send_seq(src, out, index, peer):
        @pl.when(peer != me_seq)
        def _():
            pltpu.make_async_remote_copy(
                src_ref=src,
                dst_ref=out.at[lax.rem(peer + heads - me_seq, heads)],
                send_sem=s_send.at[index],
                recv_sem=s_recv.at[index],
                device_id=(me_dp, peer),
                device_id_type=MESH,
            ).start()

        @pl.when(peer == me_seq)
        def _():
            pltpu.make_async_copy(src, out.at[0], own_sem.at[index]).start()

    def send_part(stage, out, index, part):
        def one(step, carry):
            c = lax.rem(step + 1 + me_seq // parts, per_part)
            peer = head_of(part, c)
            send_seq(stage.at[peer], out, index, peer)
            return carry

        lax.fori_loop(0, per_part, one, 0)

    def seq_total(out, index):
        return pltpu.make_async_remote_copy(
            src_ref=out.at[pl.ds(1, heads - 1)],
            dst_ref=out.at[pl.ds(1, heads - 1)],
            send_sem=s_send.at[index],
            recv_sem=s_recv.at[index],
            device_id=(me_dp, lax.rem(me_seq + 1, heads)),
            device_id_type=MESH,
        )

    def dest_block(moved, kept, j):
        return jnp.where(tab[groups + 2, j] == 1, kept.astype(F32), moved.astype(F32))

    def pass_on(pool, here, stage, out, index, part):
        for j in range(LIVE):
            kept = here[tab[groups + 1, j]]
            kept = jnp.concatenate(
                [kept[:, h * HEAD:(h + 1) * HEAD] for h in [head_of(part, c) for c in range(per_part)]], axis=1
            )
            rows32[j * TOKENS:(j + 1) * TOKENS, : per_part * HEAD] = dest_block(
                pool[part][tab[groups, j]], kept, j
            )
        for c in range(per_part):
            stage[head_of(part, c)] = rows32[:, c * HEAD:(c + 1) * HEAD].astype(BF16)
        send_part(stage, out, index, part)

    loads[0].wait()
    pack(keys_here, keys_send)
    pl.semaphore_wait(barrier, groups + heads - 2)
    for part in range(parts):
        send_dp(keys_send.at[part], keys_pool[part], part)

    loads[3].wait()
    for j in range(LIVE):
        rows32[j * TOKENS:(j + 1) * TOKENS, :] = grad_buf[j].astype(F32)
    for h in range(heads):
        grad_stage[h] = rows32[:, h * HEAD:(h + 1) * HEAD].astype(BF16)
    for part in range(parts):
        send_part(grad_stage, grad_out, 3, part)

    loads[1].wait()
    loads[2].wait()
    for b in range(blocks):
        feat32[b * TOKENS:(b + 1) * TOKENS, :] = feat_buf[b].astype(F32)
    nt = (((1,), (1,)), ((), ()))
    features = feat32[: blocks * TOKENS, :].astype(BF16)
    adapter = lax.dot_general(features, down_ref[...], nt, preferred_element_type=F32).astype(BF16)
    adapter32[: blocks * TOKENS, :] = jnp.concatenate([adapter, adapter], axis=1).astype(F32)
    up32[...] = jnp.dot(adapter, up_ref[...], preferred_element_type=F32)
    for b in range(blocks):
        query_here[b] = (query_here[b].astype(F32) + up32[b * TOKENS:(b + 1) * TOKENS, :]).astype(BF16)
        adapter_here[b] = adapter32[b * TOKENS:(b + 1) * TOKENS, :].astype(BF16)
    pack(query_here, query_send)
    for i in range(slots):
        adapter_send[i] = adapter_here[slot_source(i)]
    send_dp(adapter_send, adapter_pool, 3 * parts)
    for part in range(parts):
        send_dp(query_send.at[part], query_pool[part], parts + part)
    loads[4].wait()
    pack(values_here, values_send)
    for part in range(parts):
        send_dp(values_send.at[part], values_pool[part], 2 * parts + part)

    for i in range(slots):
        feat32[i * TOKENS:(i + 1) * TOKENS, :] = feat_buf[slot_source(i)].astype(F32)
    for k in range(groups - 1):
        feat_moving[k] = feat32[k * CAP * TOKENS:(k + 1) * CAP * TOKENS, :].astype(BF16)
    for j in range(LIVE):
        feat32[j * TOKENS:(j + 1) * TOKENS, :] = feat_buf[tab[groups + 1, j]].astype(F32)
    feat_staying[...] = feat32[:ROWS, :].astype(BF16)

    for part in range(parts):
        dp_total(keys_send.at[part], keys_pool[part], part).wait_recv()
        pass_on(keys_pool, keys_here, keys_stage, keys_out, 0, part)
    dp_total(adapter_send, adapter_pool, 3 * parts).wait_recv()
    adapter32[...] = jnp.zeros_like(adapter32)
    for j in range(LIVE):
        adapter32[j * TOKENS:(j + 1) * TOKENS, :] = dest_block(
            adapter_pool[tab[groups, j]], adapter_here[tab[groups + 1, j]], j
        )
    lane = lax.broadcasted_iota(jnp.int32, (FOLD, HEAD), 1)
    adapter_stage[...] = jnp.where(
        lane < RANK, adapter32[0:FOLD, :], adapter32[FOLD:2 * FOLD, :]
    ).astype(BF16)

    def spread(k, carry):
        send_seq(adapter_stage, adapter_out, 4, lax.rem(me_seq + k, heads))
        return carry

    lax.fori_loop(0, heads, spread, 0)
    for part in range(parts):
        dp_total(query_send.at[part], query_pool[part], parts + part).wait_recv()
        pass_on(query_pool, query_here, query_stage, query_out, 2, part)
    for part in range(parts):
        dp_total(values_send.at[part], values_pool[part], 2 * parts + part).wait_recv()
        pass_on(values_pool, values_here, values_stage, values_out, 1, part)

    for part in range(parts):
        dp_total(keys_send.at[part], keys_pool[part], part).wait_send()
        dp_total(query_send.at[part], query_pool[part], parts + part).wait_send()
        dp_total(values_send.at[part], values_pool[part], 2 * parts + part).wait_send()
    dp_total(adapter_send, adapter_pool, 3 * parts).wait_send()
    outs = (keys_out, values_out, query_out, grad_out, adapter_out)
    stages = (keys_stage, values_stage, query_stage, grad_stage, None)
    for index in (3, 0, 4, 2, 1):
        out = outs[index]
        own = adapter_stage if stages[index] is None else stages[index].at[0]
        pltpu.make_async_copy(own, out.at[0], own_sem.at[index]).wait()
        seq_total(out, index).wait_recv()
        seq_total(out, index).wait_send()


def exchange(tables, keys, values, base, grads, features, down_t, up, groups, heads):
    blocks = keys.shape[0]
    slots = (groups - 1) * CAP
    width = heads * HEAD
    parts = min(PARTS, heads)
    inputs = features.shape[2]
    vmem = pl.BlockSpec(memory_space=pltpu.VMEM)
    hbm = pl.BlockSpec(memory_space=pl.ANY)
    chunk = jax.ShapeDtypeStruct((heads, ROWS, HEAD), BF16)
    feat_rows = max(slots, LIVE, blocks) * TOKENS
    adapter_rows = max(blocks * TOKENS, 2 * FOLD)
    arriving = pltpu.VMEM((slots, TOKENS, width // parts), BF16)
    moving = pltpu.VMEM((parts, slots, TOKENS, width // parts), BF16)
    here = pltpu.VMEM((blocks, TOKENS, width), BF16)
    stage = pltpu.VMEM((heads, ROWS, HEAD), BF16)
    return pl.pallas_call(
        functools.partial(exchange_kernel, groups, heads, parts),
        out_shape=(
            chunk, chunk, chunk, chunk,
            jax.ShapeDtypeStruct((heads, FOLD, HEAD), BF16),
            jax.ShapeDtypeStruct((groups - 1, CAP * TOKENS, inputs), BF16),
            jax.ShapeDtypeStruct((ROWS, inputs), BF16),
        ),
        in_specs=[pl.BlockSpec(memory_space=pltpu.SMEM)] + [hbm] * 5 + [vmem] * 2,
        out_specs=[hbm] * 5 + [vmem] * 2,
        scratch_shapes=[arriving] * (3 * parts) + [
            pltpu.VMEM((slots, TOKENS, HEAD), BF16),
            here, here, here,
            pltpu.VMEM((blocks, TOKENS, HEAD), BF16),
            here,
            pltpu.VMEM((blocks, TOKENS, inputs), BF16),
            moving, moving, moving,
            pltpu.VMEM((slots, TOKENS, HEAD), BF16),
            stage, stage, stage, stage,
            pltpu.VMEM((FOLD, HEAD), BF16),
            pltpu.VMEM((ROWS, width), F32),
            pltpu.VMEM((feat_rows, inputs), F32),
            pltpu.VMEM((blocks * TOKENS, width), F32),
            pltpu.VMEM((adapter_rows, HEAD), F32),
            pltpu.SemaphoreType.DMA((5,)),
            pltpu.SemaphoreType.DMA((5,)),
            pltpu.SemaphoreType.DMA((3 * parts + 1,)),
            pltpu.SemaphoreType.DMA((3 * parts + 1,)),
            pltpu.SemaphoreType.DMA((5,)),
            pltpu.SemaphoreType.DMA((5,)),
        ],
        compiler_params=pltpu.CompilerParams(
            collective_id=1, has_side_effects=True, vmem_limit_bytes=VMEM_LIMIT
        ),
        name="exchange",
    )(tables, keys, values, base, grads, features, down_t, up)


def attend_kernel(
    groups, heads, tile, scale, tab, segments_ref, up_ref, query_ref, key_ref, value_ref, grad_ref, adapter_ref,
    feat_moving, feat_staying,
    down_out, up_out, log_ref,
    key_max, key_sum, value_sum, value_neg, scores, probs, dquery, logs, up_head,
    feat_recv, feat32, partial_send, partial_recv, blocks32, pieces, down_send, down_recv,
    up_send, up_recv, total_send, total_recv, whole32, share_recv,
    up_sem, s_send, s_recv, z_send, z_recv,
):
    total = heads * ROWS
    me_dp = lax.axis_index("dp")
    me_seq = lax.axis_index("seq")
    slots = (groups - 1) * CAP
    up_rows = RANK // groups
    scaling = 1.0 / math.sqrt(HEAD)
    to_exp2 = scaling * math.log2(math.e)
    nt = (((1,), (1,)), ((), ()))
    tn = (((0,), (0,)), ((), ()))
    zero = jnp.zeros((), BF16)

    def seq_copy(k, src, dst, index):
        return pltpu.make_async_remote_copy(
            src_ref=src, dst_ref=dst, send_sem=s_send.at[index], recv_sem=s_recv.at[index],
            device_id=(me_dp, k), device_id_type=MESH,
        )

    def dp_copy(k, src, dst, index):
        return pltpu.make_async_remote_copy(
            src_ref=src, dst_ref=dst, send_sem=z_send.at[index], recv_sem=z_recv.at[index],
            device_id=(k, me_seq), device_id_type=MESH,
        )

    barrier = greet_all(groups, heads, me_dp, me_seq)
    up_copy = pltpu.make_async_copy(
        up_ref.at[:, pl.ds(pl.multiple_of(me_seq * HEAD, HEAD), HEAD)], up_head, up_sem
    )
    up_copy.start()
    live_count = jnp.sum((segments_ref[...] < 1).astype(jnp.int32), axis=1, keepdims=True)

    def position(first, rows):
        token = first + lax.broadcasted_iota(jnp.int32, (rows, HEAD), 0)
        part = (token * 52429) >> 22
        rest = token - part * ROWS
        owner = (me_seq - part) & (heads - 1)
        return (rest >> 2) * (TOKENS * heads) + owner * TOKENS + (rest & 3)

    first_row = pl.multiple_of(me_seq * ROWS, 16)
    filler = key_ref[pl.ds(first_row, 16), :][0:1, :]
    lane = lax.broadcasted_iota(jnp.int32, (ROWS, HEAD), 1)
    for k in range(heads):
        at = slice(k * ROWS, (k + 1) * ROWS)
        live = position(k * ROWS, ROWS) < live_count
        rows = key_ref[at, :]
        value = jnp.where(live, value_ref[at, :], zero)
        key_max[at, :] = jnp.where(live, rows, filler)
        key_sum[at, :] = jnp.where(live, rows, zero)
        value_sum[at, 0:HEAD] = value
        value_sum[at, HEAD:] = jnp.where(live, 1.0, 0.0).astype(BF16)
        value_neg[at, 0:HEAD] = value
        value_neg[at, HEAD:] = jnp.where(lane < 3, -1.0, 0.0).astype(BF16)

    up_copy.wait()
    up = up_head[...]
    nothing = jnp.zeros((RANK, HEAD), BF16)
    to_low = jnp.concatenate([up, nothing], axis=0)
    to_high = jnp.concatenate([nothing, up], axis=0)
    filling = jnp.zeros((2 * FOLD - ROWS, HEAD), BF16)

    pl.semaphore_wait(barrier, groups + heads - 2)

    def send_features(k, carry):
        dp_copy(lax.rem(me_dp + k, groups), feat_moving.at[k - 1], feat_recv.at[k - 1], 0).start()
        return carry

    lax.fori_loop(1, groups, send_features, 0)
    lanes = lax.broadcasted_iota(jnp.int32, (tile, HEAD), 1)

    def one_tile(index, carry):
        first = pl.multiple_of(index * tile, tile)
        query = query_ref[pl.ds(first, tile), :]
        grad = grad_ref[pl.ds(first, tile), :]
        scores[...] = lax.dot_general(query, key_max[...], nt, preferred_element_type=F32)
        maximum = jnp.max(scores[...], axis=1, keepdims=True)
        probs[...] = jnp.exp2((scores[...] - maximum) * to_exp2).astype(BF16)
        summed = jnp.dot(probs[...], value_sum[...], preferred_element_type=F32)
        norm = summed[:, HEAD:]
        inverse = 1.0 / norm
        delta = jnp.sum(grad.astype(F32) * summed[:, :HEAD], axis=1, keepdims=True) * inverse
        high = delta.astype(BF16)
        middle = (delta - high.astype(F32)).astype(BF16)
        low = (delta - high.astype(F32) - middle.astype(F32)).astype(BF16)
        split = jnp.where(lanes == 0, high, jnp.where(lanes == 1, middle, jnp.where(lanes == 2, low, zero)))
        wide = jnp.concatenate([grad, split], axis=1)
        dprob = lax.dot_general(wide, value_neg[...], nt, preferred_element_type=F32)
        dscore = (probs[...].astype(F32) * dprob).astype(BF16)
        result = jnp.dot(dscore, key_sum[...], preferred_element_type=F32) * (inverse * scaling)
        live = position(first, tile) < live_count
        result = jnp.where(live, result, 0.0).astype(BF16)
        dquery[pl.ds(first, tile), :] = result
        logs[pl.ds(first, tile), :] = jnp.where(live, maximum * scaling + jnp.log(norm), 0.0)
        for c in range(tile // ROWS):
            k = index * (tile // ROWS) + c
            first_part = result[c * ROWS:c * ROWS + FOLD]
            second_part = jnp.concatenate([result[c * ROWS + FOLD:(c + 1) * ROWS], filling], axis=0)
            partial_send[k] = (
                lax.dot_general(first_part, to_low, nt, preferred_element_type=F32)
                + lax.dot_general(second_part, to_high, nt, preferred_element_type=F32)
            ).astype(BF16)

            @pl.when(k > 0)
            def _():
                seq_copy(
                    lax.rem(me_seq + heads - k, heads), partial_send.at[k], partial_recv.at[k - 1], 0
                ).start()

        return carry

    lax.fori_loop(0, total // tile, one_tile, 0)

    up_total = jnp.zeros((RANK, HEAD), F32)
    for k in range(heads):
        first_part = dquery[k * ROWS:k * ROWS + FOLD, :]
        second_part = jnp.concatenate([dquery[k * ROWS + FOLD:(k + 1) * ROWS, :], filling], axis=0)
        folded = adapter_ref[k]
        up_total = up_total + lax.dot_general(folded, first_part, tn, preferred_element_type=F32)[:RANK]
        up_total = up_total + lax.dot_general(folded, second_part, tn, preferred_element_type=F32)[RANK:]
    up_send[...] = jnp.zeros_like(up_send)
    for d in range(groups):
        up_send[d, 0:up_rows, :] = up_total[d * up_rows:(d + 1) * up_rows, :]

    def send_up(k, carry):
        peer = lax.rem(me_dp + k, groups)
        dp_copy(peer, up_send.at[peer], up_recv.at[k - 1], 1).start()
        return carry

    lax.fori_loop(1, groups, send_up, 0)

    def dp_total(like, index):
        return dp_copy(lax.rem(me_dp + 1, groups), like, like, index)

    dp_total(feat_recv, 0).wait_recv()
    for k in range(groups - 1):
        feat32[k * CAP * TOKENS:(k + 1) * CAP * TOKENS, :] = feat_recv[k].astype(F32)
    moved_rows = feat32[...].astype(BF16)

    partial_total = seq_copy(lax.rem(me_seq + 1, heads), partial_send.at[pl.ds(1, heads - 1)], partial_recv, 0)
    partial_total.wait_recv()
    folded = partial_send[0].astype(F32)
    for k in range(heads - 1):
        folded = folded + partial_recv[k].astype(F32)
    turned = pltpu.roll(folded, RANK, 1)
    for j in range(LIVE):
        row = j * TOKENS
        half = folded if row < FOLD else turned
        row = row if row < FOLD else row - FOLD
        blocks32[j] = half[row:row + TOKENS, :]
    blocks32[LIVE] = jnp.zeros((TOKENS, HEAD), F32)
    for k in range(1, groups):
        origin = lax.rem(me_dp + groups - k, groups)
        for r in range(CAP):
            row = ((k - 1) * CAP + r) * TOKENS
            pieces[row:row + TOKENS, :] = blocks32[tab[origin, CAP + r]]
    for j in range(LIVE):
        stays = tab[groups + 2, j].astype(F32)
        pieces[(slots + j) * TOKENS:(slots + j + 1) * TOKENS, :] = blocks32[j] * stays
    own_lane = lax.broadcasted_iota(jnp.int32, pieces.shape, 1)
    grads = pieces[...]
    doubled = jnp.where(own_lane < RANK, grads, pltpu.roll(grads, RANK, 1)).astype(BF16)
    down = lax.dot_general(doubled[:slots * TOKENS], moved_rows, tn, preferred_element_type=F32)
    down = down + lax.dot_general(doubled[slots * TOKENS:], feat_staying[...], tn, preferred_element_type=F32)
    down = down.T
    fold_lane = lax.broadcasted_iota(jnp.int32, (FOLD, HEAD), 1)
    for h in range(heads):
        first = down[h * ROWS:h * ROWS + FOLD, :]
        second = jnp.concatenate(
            [down[h * ROWS + FOLD:(h + 1) * ROWS, :], jnp.zeros((2 * FOLD - ROWS, HEAD), F32)], axis=0
        )
        down_send[h] = jnp.where(fold_lane < RANK, first, second).astype(BF16)

    def send_down(k, carry):
        peer = lax.rem(me_seq + k, heads)
        seq_copy(peer, down_send.at[peer], down_recv.at[k - 1], 1).start()
        return carry

    lax.fori_loop(1, heads, send_down, 0)

    dp_total(up_recv, 1).wait_recv()
    up_sum = up_send[me_dp]
    for k in range(groups - 1):
        up_sum = up_sum + up_recv[k]
    total_send[...] = up_sum * scale

    def send_total(k, carry):
        dp_copy(lax.rem(me_dp + k, groups), total_send, total_recv.at[k - 1], 2).start()
        return carry

    lax.fori_loop(1, groups, send_total, 0)
    gathered = jnp.zeros((ROWS, HEAD), F32)
    row = lax.broadcasted_iota(jnp.int32, (ROWS, HEAD), 0)
    for k in range(heads):
        owner = (me_seq - k) & (heads - 1)
        column = owner * TOKENS + (row & 3)
        gathered = gathered + jnp.where(lane == column, logs[k * ROWS:(k + 1) * ROWS, :], 0.0)
    pick = lax.broadcasted_iota(jnp.int32, log_ref.shape[:1] + (ROWS,), 1) >> 2
    pick = (pick == lax.broadcasted_iota(jnp.int32, pick.shape, 0)).astype(F32)
    log_ref[...] = jnp.dot(pick, gathered, preferred_element_type=F32, precision=lax.Precision.HIGHEST)
    dp_total(total_recv, 2).wait_recv()
    whole32[me_dp] = total_send[...]
    for k in range(1, groups):
        whole32[lax.rem(me_dp + groups - k, groups)] = total_recv[k - 1]
    for d in range(groups):
        up_out[d * up_rows:(d + 1) * up_rows, :] = whole32[d, 0:up_rows, :]

    down_total = seq_copy(lax.rem(me_seq + 1, heads), down_send.at[pl.ds(0, heads - 1)], down_recv, 1)
    down_total.wait_recv()
    share = down_send[me_seq].astype(F32)
    for k in range(heads - 1):
        share = share + down_recv[k].astype(F32)
    share_recv[0] = share.astype(BF16)

    def send_share(k, carry):
        dp_copy(lax.rem(me_dp + k, groups), share_recv.at[0], share_recv.at[k], 3).start()
        return carry

    lax.fori_loop(1, groups, send_share, 0)
    share_total = dp_total(share_recv.at[pl.ds(1, groups - 1)], 3)
    share_total.wait_recv()
    share = jnp.zeros((FOLD, HEAD), F32)
    for d in range(groups):
        share = share + share_recv[lax.rem(me_dp + groups - d, groups)].astype(F32)
    share = share * scale
    turned = pltpu.roll(share, RANK, 1)
    whole = jnp.concatenate(
        [share, turned[:ROWS - FOLD], jnp.zeros((HEAD - ROWS, HEAD), F32)], axis=0
    )
    down_out[...] = whole.T[:RANK, :ROWS]

    dp_total(feat_recv, 0).wait_send()
    dp_total(up_recv, 1).wait_send()
    dp_total(total_recv, 2).wait_send()
    share_total.wait_send()
    partial_total.wait_send()
    down_total.wait_send()


def attend(
    tables, segments, up, query, keys, values, grads, adapter, feat_moving, feat_staying, scale, blocks, groups, heads
):
    total = heads * ROWS
    tile = 4 * ROWS if heads % 4 == 0 else 2 * ROWS
    slots = (groups - 1) * CAP
    inputs = feat_staying.shape[1]
    vmem = pl.BlockSpec(memory_space=pltpu.VMEM)
    up_tile = max(8, RANK // groups)
    folded = (FOLD, HEAD)
    return pl.pallas_call(
        functools.partial(attend_kernel, groups, heads, tile, scale),
        out_shape=(
            jax.ShapeDtypeStruct((RANK, ROWS), F32),
            jax.ShapeDtypeStruct((RANK, HEAD), F32),
            jax.ShapeDtypeStruct((blocks, HEAD), F32),
        ),
        in_specs=[pl.BlockSpec(memory_space=pltpu.SMEM), vmem, pl.BlockSpec(memory_space=pl.ANY)] + [vmem] * 7,
        out_specs=[vmem] * 3,
        scratch_shapes=[
            pltpu.VMEM((total, HEAD), BF16),
            pltpu.VMEM((total, HEAD), BF16),
            pltpu.VMEM((total, 2 * HEAD), BF16),
            pltpu.VMEM((total, 2 * HEAD), BF16),
            pltpu.VMEM((tile, total), F32),
            pltpu.VMEM((tile, total), BF16),
            pltpu.VMEM((total, HEAD), BF16),
            pltpu.VMEM((total, HEAD), F32),
            pltpu.VMEM((RANK, HEAD), BF16),
            pltpu.VMEM(feat_moving.shape, BF16),
            pltpu.VMEM((slots * TOKENS, inputs), F32),
            pltpu.VMEM((heads,) + folded, BF16),
            pltpu.VMEM((heads - 1,) + folded, BF16),
            pltpu.VMEM((LIVE + 1, TOKENS, HEAD), F32),
            pltpu.VMEM(((slots + LIVE) * TOKENS, HEAD), F32),
            pltpu.VMEM((heads,) + folded, BF16),
            pltpu.VMEM((heads - 1,) + folded, BF16),
            pltpu.VMEM((groups, up_tile, HEAD), F32),
            pltpu.VMEM((groups - 1, up_tile, HEAD), F32),
            pltpu.VMEM((up_tile, HEAD), F32),
            pltpu.VMEM((groups - 1, up_tile, HEAD), F32),
            pltpu.VMEM((groups, up_tile, HEAD), F32),
            pltpu.VMEM((groups,) + folded, BF16),
            pltpu.SemaphoreType.DMA,
            pltpu.SemaphoreType.DMA((2,)),
            pltpu.SemaphoreType.DMA((2,)),
            pltpu.SemaphoreType.DMA((4,)),
            pltpu.SemaphoreType.DMA((4,)),
        ],
        compiler_params=pltpu.CompilerParams(
            collective_id=2, has_side_effects=True, vmem_limit_bytes=VMEM_LIMIT
        ),
        name="attend",
    )(tables, segments, up, query, keys, values, grads, adapter, feat_moving, feat_staying)


def per_device(
    features, frozen_query_weight, source_keys, source_values, output_gradient,
    adapter_down_weight, adapter_up_weight, source_block_plan, segments,
):
    groups = lax.axis_size("dp")
    heads = lax.axis_size("seq")
    length = segments.shape[1]
    blocks = source_keys.shape[1]
    tables = block_tables(source_block_plan, groups)
    keys, values, query, grads, adapter, feat_moving, feat_staying = exchange(
        tables, source_keys[0], source_values[0], frozen_query_weight[0], output_gradient[0], features[0],
        adapter_down_weight.T, adapter_up_weight, groups, heads,
    )
    total = heads * ROWS
    scale = 4.0 / math.sqrt(groups * length)
    down, up, logs = attend(
        tables, segments, adapter_up_weight, query.reshape(total, HEAD), keys.reshape(total, HEAD),
        values.reshape(total, HEAD), grads.reshape(total, HEAD), adapter, feat_moving, feat_staying,
        scale, blocks, groups, heads,
    )
    log_norm = logs[:, : TOKENS * heads].reshape(1, 1, length)
    return (down.T, up, log_norm)


def solution(mesh):
    in_specs = (
        P("dp", None, "seq", None),
        P("dp", None, "seq", None),
        P("dp", None, "seq", None),
        P("dp", None, "seq", None),
        P("dp", None, "seq", None),
        P(),
        P(),
        P(),
        P("dp", None),
    )
    out_specs = (P("seq", None), P(None, "seq"), P("dp", "seq", None))
    return jax.shard_map(
        per_device, mesh=mesh, in_specs=in_specs, out_specs=out_specs, check_vma=False
    )
```

time: 206 us -> 160 us (0.78); the launches traced: 204 us -> 160 us
  Pallas kernels: 193 us -> 157 us
  local copies, waits for them, and re-layouts: 6.72 us -> 2.72 us
  other arithmetic: 3.54 us -> 0 us
    pallas_call x3, Pallas kernels: 193 us -> 157 us  [the longest x1 93.8 us: exchange(): pl.pallas_call(functools.partial(exchange_kernel, groups, heads, parts),...]
where the time goes in v2:
time: 160 us
  Pallas kernels  157 us (98%)
  local copies, waits for them, and re-layouts  2.72 us (2%)
    pallas_call x1, Pallas kernels, exchange(): pl.pallas_call(functools.partial(exchange_kernel, groups, heads, parts),...  93.8 us
    pallas_call x1, Pallas kernels, attend(): pl.pallas_call(functools.partial(attend_kernel, groups, heads, tile, scal...  61.3 us

profile of v2, /device:TPU:1, one launch (start us, length us, event | category | flops | bytes accessed | tf_op | source)
XLA Modules:
  0.0 160.0 jit_solution(5487350804241888199)
XLA Ops:
  0.6 1.5 tables.1.tab
  2.1 93.8 %exchange.1 = (bf16[32,80,128]{2,1,0:T(8,128)(2,1)}, bf16[32,80,128]{2,1,0:T(8,128)(2,1)}, bf16[32,80,128]{2,1,0:T(8,128)(2,1)}, bf16[32,80,128]{2,1,0:T(8,128)(...) custom-call(s32[24,128]{1,0:T(8,128)} %tables.1.tab, ...), custom_call_target="tpu_custom_call" | custom-call | tf_op jit(solution)/shard_map/exchange/pallas_call | solution.py:313
  96.0 61.3 %attend.1 = (f32[64,80]{1,0:T(8,128)}, f32[64,128]{1,0:T(8,128)}, f32[32,128]{1,0:T(8,128)}) custom-call(s32[24,128]{1,0:T(8,128)} %tables.1.tab, s32[1,4096]{1,0:T(1,128)} %segments_ref.1, bf16[64,4096]{1,0:T(8,128)(2,1)} %up_ref.3, bf16[2560,128]{1,0:T(8,128)(2,1)} %bitcast.19, bf16[2560,128]{1,0:T(8,128)(2,1)} %bitcast.17, bf16[2560,128]{1,0:T(8,128)(2,1)} %bitcast.18, ...), custom_call_target="tpu_custom_call" | custom-call | tf_op jit(solution)/shard_map/attend/pallas_call | solution.py:606
  157.2 0.0 copy-start
  157.3 1.4 copy.15
  158.6 0.0 copy-done
  158.6 0.0 copy-start.1
  158.6 0.6 copy.16
  159.3 0.1 copy-done.1
  159.4 0.6 copy.17
Async XLA Ops:
  157.2 1.4 copy-start
  158.6 0.7 copy-start.1

commit v3 on v2

v3 whole, which is shorter than its diff:
```python
import functools
import math

import jax
import jax.numpy as jnp
from jax import lax
from jax.experimental import pallas as pl
from jax.experimental.pallas import tpu as pltpu
from jax.sharding import PartitionSpec as P

CAP = 2
HEAD = 128
RANK = 64
TOKENS = 4
LIVE = 20
ROWS = LIVE * TOKENS
PARTS = 4
FOLD = 48
MESH = pl.DeviceIdType.MESH
BF16 = jnp.bfloat16
F32 = jnp.float32
VMEM_LIMIT = 56 * 1024 * 1024


def tables_kernel(groups, plan_ref, tab_ref):
    group = lax.axis_index("dp")
    blocks = plan_ref.shape[1]
    shift = blocks.bit_length() - 1
    plan = plan_ref[...]
    source, local = plan >> shift, plan & (blocks - 1)
    row = lax.broadcasted_iota(jnp.int32, (groups, blocks), 0)
    place = lax.broadcasted_iota(jnp.int32, (groups, blocks), 1)
    live = place < LIVE
    first = lax.broadcasted_iota(jnp.int32, (blocks, blocks), 0)
    second = lax.broadcasted_iota(jnp.int32, (blocks, blocks), 1)
    match = live & (source == group)
    rank = jnp.dot(match.astype(F32), (first < second).astype(F32), preferred_element_type=F32)

    def column(chosen, value):
        return jnp.sum(jnp.where(chosen, value, 0), axis=1, keepdims=True)

    send = [column(match & (rank == r), local) for r in range(CAP)]
    own = jnp.sum(jnp.where(row == group, plan, 0), axis=0, keepdims=True)
    own_source, own_local = own >> shift, own & (blocks - 1)
    down_column = jnp.sum(jnp.where(first == second, own_source, 0), axis=1, keepdims=True)
    same = (down_column == own_source) & (first < second)
    own_rank = jnp.sum(same.astype(jnp.int32), axis=0, keepdims=True)
    back = [
        LIVE + column(live & (own_source == row) & (own_rank == r), place - LIVE) for r in range(CAP)
    ]
    stays = own_source == group
    distance = (group - own_source + groups) & (groups - 1)
    take = jnp.where(stays, 0, (distance - 1) * CAP + own_rank)
    tab_ref[...] = jnp.zeros_like(tab_ref)
    for at, part in enumerate(send + back):
        tab_ref[0:groups, at:at + 1] = part
    tab_ref[groups:groups + 1, 0:blocks] = take
    tab_ref[groups + 1:groups + 2, 0:blocks] = jnp.where(stays, own_local, 0)
    tab_ref[groups + 2:groups + 3, 0:blocks] = stays.astype(jnp.int32)


def block_tables(plan, groups):
    vmem = pl.BlockSpec(memory_space=pltpu.VMEM)
    return pl.pallas_call(
        functools.partial(tables_kernel, groups),
        out_shape=jax.ShapeDtypeStruct((24, HEAD), jnp.int32),
        in_specs=[vmem],
        out_specs=vmem,
        name="tables",
    )(plan)


def greet_all(groups, heads, me_dp, me_seq):
    barrier = pltpu.get_barrier_semaphore()

    def greet_dp(k, carry):
        pl.semaphore_signal(
            barrier, inc=1, device_id=(lax.rem(me_dp + k, groups), me_seq), device_id_type=MESH
        )
        return carry

    def greet_seq(k, carry):
        pl.semaphore_signal(
            barrier, inc=1, device_id=(me_dp, lax.rem(me_seq + k, heads)), device_id_type=MESH
        )
        return carry

    lax.fori_loop(1, groups, greet_dp, 0)
    lax.fori_loop(1, heads, greet_seq, 0)
    return barrier


def whole_kernel(
    groups, heads, parts, scale, tab, segments_ref, down_ref, up_ref, keys_in, values_in, base_in, grad_in, feat_in,
    down_out, up_out, log_ref,
    *scratch,
):
    keys_pool, values_pool, query_pool = (scratch[n * parts:(n + 1) * parts] for n in range(3))
    (
        adapter_pool,
        keys_here, values_here, query_here, adapter_here, grad_buf, feat_buf,
        keys_send, values_send, query_send, adapter_send,
        keys_stage, values_stage, query_stage, grad_stage, adapter_stage, rows32, feat32, up32, adapter32,
        keys_got, values_got, query_got, grad_got, adapter_got, feat_moving, feat_staying,
        key_max, key_sum, value_sum, value_neg, scores, probs, dquery, logs, up_head,
        feat_recv, partial_send, partial_recv, blocks32, pieces, down_send, down_recv,
        up_send, up_recv, total_send, total_recv, whole32, share_recv,
        up_sem, load_sem, own_sem, z_send, z_recv, s_send, s_recv,
    ) = scratch[3 * parts:]
    me_dp = lax.axis_index("dp")
    me_seq = lax.axis_index("seq")
    slots = (groups - 1) * CAP
    blocks = keys_in.shape[0]
    total = heads * ROWS
    tile = total // parts
    step = 256 if total % 256 == 0 else total
    per_tile = tile // ROWS
    up_rows = RANK // groups
    seq_base = 5
    dp_base = 3 * parts + 1
    scaling = 1.0 / math.sqrt(HEAD)
    to_exp2 = scaling * math.log2(math.e)
    nt = (((1,), (1,)), ((), ()))
    tn = (((0,), (0,)), ((), ()))
    zero = jnp.zeros((), BF16)
    per_part = heads // parts

    def head_of(part, c):
        return c * parts + ((part - c) & (parts - 1))

    def slot_source(i):
        return tab[lax.rem(me_dp + 1 + i // CAP, groups), i % CAP]

    loads = [
        pltpu.make_async_copy(keys_in, keys_here, load_sem.at[0]),
        pltpu.make_async_copy(base_in, query_here, load_sem.at[1]),
        pltpu.make_async_copy(feat_in, feat_buf, load_sem.at[2]),
        pltpu.make_async_copy(grad_in, grad_buf, load_sem.at[3]),
        pltpu.make_async_copy(values_in, values_here, load_sem.at[4]),
    ]
    for copy in loads:
        copy.start()
    barrier = greet_all(groups, heads, me_dp, me_seq)
    up_copy = pltpu.make_async_copy(
        up_ref.at[:, pl.ds(pl.multiple_of(me_seq * HEAD, HEAD), HEAD)], up_head, up_sem
    )
    up_copy.start()

    def pack(here, send):
        for i in range(slots):
            block = here[slot_source(i)]
            for part in range(parts):
                for c in range(per_part):
                    h = head_of(part, c)
                    send[part, i, :, c * HEAD:(c + 1) * HEAD] = block[:, h * HEAD:(h + 1) * HEAD]

    def send_dp(send, pool, index):
        def one(k, carry):
            pltpu.make_async_remote_copy(
                src_ref=send.at[pl.ds((k - 1) * CAP, CAP)],
                dst_ref=pool.at[pl.ds((k - 1) * CAP, CAP)],
                send_sem=z_send.at[index],
                recv_sem=z_recv.at[index],
                device_id=(lax.rem(me_dp + k, groups), me_seq),
                device_id_type=MESH,
            ).start()
            return carry

        lax.fori_loop(1, groups, one, 0)

    def dp_part(send, pool, index):
        return pltpu.make_async_remote_copy(
            src_ref=send,
            dst_ref=pool,
            send_sem=z_send.at[index],
            recv_sem=z_recv.at[index],
            device_id=(lax.rem(me_dp + 1, groups), me_seq),
            device_id_type=MESH,
        )

    def send_seq(src, out, index, peer):
        @pl.when(peer != me_seq)
        def _():
            pltpu.make_async_remote_copy(
                src_ref=src,
                dst_ref=out.at[lax.rem(peer + heads - me_seq, heads)],
                send_sem=s_send.at[index],
                recv_sem=s_recv.at[index],
                device_id=(me_dp, peer),
                device_id_type=MESH,
            ).start()

        @pl.when(peer == me_seq)
        def _():
            pltpu.make_async_copy(src, out.at[0], own_sem.at[index]).start()

    def send_part(stage, out, index, part):
        def one(step, carry):
            c = lax.rem(step + 1 + me_seq // parts, per_part)
            peer = head_of(part, c)
            send_seq(stage.at[peer], out, index, peer)
            return carry

        lax.fori_loop(0, per_part, one, 0)

    def seq_total(out, index):
        return pltpu.make_async_remote_copy(
            src_ref=out.at[pl.ds(1, heads - 1)],
            dst_ref=out.at[pl.ds(1, heads - 1)],
            send_sem=s_send.at[index],
            recv_sem=s_recv.at[index],
            device_id=(me_dp, lax.rem(me_seq + 1, heads)),
            device_id_type=MESH,
        )

    def dest_block(moved, kept, j):
        return jnp.where(tab[groups + 2, j] == 1, kept.astype(F32), moved.astype(F32))

    def pass_on(pool, here, stage, out, index, part):
        for j in range(LIVE):
            kept = here[tab[groups + 1, j]]
            kept = jnp.concatenate(
                [kept[:, h * HEAD:(h + 1) * HEAD] for h in [head_of(part, c) for c in range(per_part)]], axis=1
            )
            rows32[j * TOKENS:(j + 1) * TOKENS, : per_part * HEAD] = dest_block(
                pool[part][tab[groups, j]], kept, j
            )
        for c in range(per_part):
            stage[head_of(part, c)] = rows32[:, c * HEAD:(c + 1) * HEAD].astype(BF16)
        send_part(stage, out, index, part)

    loads[0].wait()
    pack(keys_here, keys_send)
    pl.semaphore_wait(barrier, groups + heads - 2)
    for part in range(parts):
        send_dp(keys_send.at[part], keys_pool[part], part)

    loads[3].wait()
    for j in range(LIVE):
        rows32[j * TOKENS:(j + 1) * TOKENS, :] = grad_buf[j].astype(F32)
    for h in range(heads):
        grad_stage[h] = rows32[:, h * HEAD:(h + 1) * HEAD].astype(BF16)
    for part in range(parts):
        send_part(grad_stage, grad_got, 3, part)

    loads[1].wait()
    loads[2].wait()
    for b in range(blocks):
        feat32[b * TOKENS:(b + 1) * TOKENS, :] = feat_buf[b].astype(F32)
    features = feat32[: blocks * TOKENS, :].astype(BF16)
    adapter = lax.dot_general(features, down_ref[...], nt, preferred_element_type=F32).astype(BF16)
    adapter32[: blocks * TOKENS, :] = jnp.concatenate([adapter, adapter], axis=1).astype(F32)
    up32[...] = jnp.dot(adapter, up_ref[...], preferred_element_type=F32)
    for b in range(blocks):
        query_here[b] = (query_here[b].astype(F32) + up32[b * TOKENS:(b + 1) * TOKENS, :]).astype(BF16)
        adapter_here[b] = adapter32[b * TOKENS:(b + 1) * TOKENS, :].astype(BF16)
    pack(query_here, query_send)
    for i in range(slots):
        adapter_send[i] = adapter_here[slot_source(i)]
    send_dp(adapter_send, adapter_pool, 3 * parts)
    for part in range(parts):
        send_dp(query_send.at[part], query_pool[part], parts + part)
    loads[4].wait()
    pack(values_here, values_send)
    for part in range(parts):
        send_dp(values_send.at[part], values_pool[part], 2 * parts + part)

    for i in range(slots):
        feat32[i * TOKENS:(i + 1) * TOKENS, :] = feat_buf[slot_source(i)].astype(F32)
    for k in range(groups - 1):
        feat_moving[k] = feat32[k * CAP * TOKENS:(k + 1) * CAP * TOKENS, :].astype(BF16)
    for j in range(LIVE):
        feat32[j * TOKENS:(j + 1) * TOKENS, :] = feat_buf[tab[groups + 1, j]].astype(F32)
    feat_staying[...] = feat32[:ROWS, :].astype(BF16)

    def take_part(send, pool, here, stage, got, index, order, part):
        dp_part(send.at[part], pool[part], order * parts + part).wait_recv()
        pass_on(pool, here, stage, got, index, part)

    def position(first, rows):
        token = first + lax.broadcasted_iota(jnp.int32, (rows, HEAD), 0)
        part = (token * 52429) >> 22
        rest = token - part * ROWS
        owner = (me_seq - part) & (heads - 1)
        return (rest >> 2) * (TOKENS * heads) + owner * TOKENS + (rest & 3)

    live_count = jnp.sum((segments_ref[...] < 1).astype(jnp.int32), axis=1, keepdims=True)
    lane80 = lax.broadcasted_iota(jnp.int32, (ROWS, HEAD), 1)
    for part in range(parts):
        take_part(keys_send, keys_pool, keys_here, keys_stage, keys_got, 0, 0, part)
    dp_part(adapter_send, adapter_pool, 3 * parts).wait_recv()
    adapter32[...] = jnp.zeros_like(adapter32)
    for j in range(LIVE):
        adapter32[j * TOKENS:(j + 1) * TOKENS, :] = dest_block(
            adapter_pool[tab[groups, j]], adapter_here[tab[groups + 1, j]], j
        )
    lane = lax.broadcasted_iota(jnp.int32, (FOLD, HEAD), 1)
    adapter_stage[...] = jnp.where(
        lane < RANK, adapter32[0:FOLD, :], adapter32[FOLD:2 * FOLD, :]
    ).astype(BF16)

    def spread(k, carry):
        send_seq(adapter_stage, adapter_got, 4, lax.rem(me_seq + k, heads))
        return carry

    lax.fori_loop(0, heads, spread, 0)
    for k in range(heads):
        at = slice(k * ROWS, (k + 1) * ROWS)
        live = position(k * ROWS, ROWS) < live_count
        value_sum[at, HEAD:] = jnp.where(live, 1.0, 0.0).astype(BF16)
        value_neg[at, HEAD:] = jnp.where(lane80 < 3, -1.0, 0.0).astype(BF16)
    for part in range(parts):
        if part == parts // 2:
            seq_total(keys_got, 0).wait_recv()
            pltpu.make_async_copy(keys_stage.at[0], keys_got.at[0], own_sem.at[0]).wait()
            filler = keys_got[me_seq][0:1, :]
            for k in range(heads):
                at = slice(k * ROWS, (k + 1) * ROWS)
                live = position(k * ROWS, ROWS) < live_count
                rows = keys_got[k]
                key_max[at, :] = jnp.where(live, rows, filler)
                key_sum[at, :] = jnp.where(live, rows, zero)
        take_part(query_send, query_pool, query_here, query_stage, query_got, 2, 1, part)

    tops = []

    def score_tile(t):
        query = query_got[t * per_tile:(t + 1) * per_tile].reshape(tile, HEAD)
        top = None
        for c in range(0, total, step):
            part_scores = lax.dot_general(query, key_max[c:c + step, :], nt, preferred_element_type=F32)
            scores[:, c:c + step] = part_scores
            for b in range(0, step, HEAD):
                piece = part_scores[:, b:b + HEAD]
                top = piece if top is None or piece.shape != top.shape else jnp.maximum(top, piece)
        top = jnp.max(top if step % HEAD == 0 else scores[...], axis=1, keepdims=True)
        for c in range(0, total, step):
            probs[t * tile:(t + 1) * tile, c:c + step] = jnp.exp2(
                (scores[:, c:c + step] - top) * to_exp2
            ).astype(BF16)
        logs[t * tile:(t + 1) * tile, :] = jnp.broadcast_to(top * scaling, (tile, HEAD))

    def dp_copy(k, src, dst, index):
        return pltpu.make_async_remote_copy(
            src_ref=src, dst_ref=dst, send_sem=z_send.at[dp_base + index], recv_sem=z_recv.at[dp_base + index],
            device_id=(k, me_seq), device_id_type=MESH,
        )

    def seq_copy(k, src, dst, index):
        return pltpu.make_async_remote_copy(
            src_ref=src, dst_ref=dst, send_sem=s_send.at[seq_base + index], recv_sem=s_recv.at[seq_base + index],
            device_id=(me_dp, k), device_id_type=MESH,
        )

    def send_features(k, carry):
        dp_copy(lax.rem(me_dp + k, groups), feat_moving.at[k - 1], feat_recv.at[k - 1], 0).start()
        return carry

    for part in range(parts):
        take_part(values_send, values_pool, values_here, values_stage, values_got, 1, 2, part)
        if part == 0:
            seq_total(query_got, 2).wait_recv()
            pltpu.make_async_copy(query_stage.at[0], query_got.at[0], own_sem.at[2]).wait()
        if part == parts - 1:
            lax.fori_loop(1, groups, send_features, 0)
        score_tile(part)

    up_copy.wait()
    up = up_head[...]
    nothing = jnp.zeros((RANK, HEAD), BF16)
    to_low = jnp.concatenate([up, nothing], axis=0)
    to_high = jnp.concatenate([nothing, up], axis=0)
    filling = jnp.zeros((2 * FOLD - ROWS, HEAD), BF16)
    lanes = lax.broadcasted_iota(jnp.int32, (tile, HEAD), 1)

    seq_total(grad_got, 3).wait_recv()
    pltpu.make_async_copy(grad_stage.at[0], grad_got.at[0], own_sem.at[3]).wait()
    seq_total(values_got, 1).wait_recv()
    pltpu.make_async_copy(values_stage.at[0], values_got.at[0], own_sem.at[1]).wait()
    for k in range(heads):
        at = slice(k * ROWS, (k + 1) * ROWS)
        value = jnp.where(position(k * ROWS, ROWS) < live_count, values_got[k], zero)
        value_sum[at, 0:HEAD] = value
        value_neg[at, 0:HEAD] = value

    state = [dict() for _ in range(parts)]

    def attend_step(t, c):
        own = state[t]
        add = jnp.dot(
            probs[t * tile:(t + 1) * tile, c:c + step], value_sum[c:c + step, :], preferred_element_type=F32
        )
        own["sum"] = add if c == 0 else own["sum"] + add
        if c + step == total:
            norm = own["sum"][:, HEAD:]
            inverse = 1.0 / norm
            grad = grad_got[t * per_tile:(t + 1) * per_tile].reshape(tile, HEAD)
            delta = jnp.sum(grad.astype(F32) * own["sum"][:, :HEAD], axis=1, keepdims=True) * inverse
            high = delta.astype(BF16)
            middle = (delta - high.astype(F32)).astype(BF16)
            low = (delta - high.astype(F32) - middle.astype(F32)).astype(BF16)
            split = jnp.where(lanes == 0, high, jnp.where(lanes == 1, middle, jnp.where(lanes == 2, low, zero)))
            own["wide"] = jnp.concatenate([grad, split], axis=1)
            own["factor"] = inverse * scaling
            at = slice(t * tile, (t + 1) * tile)
            own["live"] = position(t * tile, tile) < live_count
            logs[at, :] = jnp.where(own["live"], logs[at, :] + jnp.log(norm), 0.0)

    def gradient_step(t, c):
        own = state[t]
        dprob = lax.dot_general(own["wide"], value_neg[c:c + step, :], nt, preferred_element_type=F32)
        dscore = (probs[t * tile:(t + 1) * tile, c:c + step].astype(F32) * dprob).astype(BF16)
        add = jnp.dot(dscore, key_sum[c:c + step, :], preferred_element_type=F32)
        own["grad"] = add if c == 0 else own["grad"] + add
        if c + step == total:
            result = jnp.where(own["live"], own["grad"] * own["factor"], 0.0).astype(BF16)
            dquery[t * tile:(t + 1) * tile, :] = result
            for i in range(per_tile):
                k = t * per_tile + i
                first_part = result[i * ROWS:i * ROWS + FOLD]
                second_part = jnp.concatenate([result[i * ROWS + FOLD:(i + 1) * ROWS], filling], axis=0)
                partial_send[k] = (
                    lax.dot_general(first_part, to_low, nt, preferred_element_type=F32)
                    + lax.dot_general(second_part, to_high, nt, preferred_element_type=F32)
                ).astype(BF16)
                if k > 0:
                    seq_copy(
                        lax.rem(me_seq + heads - k, heads), partial_send.at[k], partial_recv.at[k - 1], 0
                    ).start()

    for t in range(parts + 1):
        for c in range(0, total, step):
            if t < parts:
                attend_step(t, c)
            if t > 0:
                gradient_step(t - 1, c)

    seq_total(adapter_got, 4).wait_recv()
    pltpu.make_async_copy(adapter_stage, adapter_got.at[0], own_sem.at[4]).wait()
    up_total = jnp.zeros((RANK, HEAD), F32)
    for k in range(heads):
        first_part = dquery[k * ROWS:k * ROWS + FOLD, :]
        second_part = jnp.concatenate([dquery[k * ROWS + FOLD:(k + 1) * ROWS, :], filling], axis=0)
        folded = adapter_got[k]
        up_total = up_total + lax.dot_general(folded, first_part, tn, preferred_element_type=F32)[:RANK]
        up_total = up_total + lax.dot_general(folded, second_part, tn, preferred_element_type=F32)[RANK:]
    up_send[...] = jnp.zeros_like(up_send)
    for d in range(groups):
        up_send[d, 0:up_rows, :] = up_total[d * up_rows:(d + 1) * up_rows, :]

    def send_up(k, carry):
        peer = lax.rem(me_dp + k, groups)
        dp_copy(peer, up_send.at[peer], up_recv.at[k - 1], 1).start()
        return carry

    lax.fori_loop(1, groups, send_up, 0)

    def dp_total(like, index):
        return dp_copy(lax.rem(me_dp + 1, groups), like, like, index)

    dp_total(feat_recv, 0).wait_recv()
    for k in range(groups - 1):
        feat32[k * CAP * TOKENS:(k + 1) * CAP * TOKENS, :] = feat_recv[k].astype(F32)
    moved_rows = feat32[: slots * TOKENS, :].astype(BF16)

    partial_total = seq_copy(lax.rem(me_seq + 1, heads), partial_send.at[pl.ds(1, heads - 1)], partial_recv, 0)
    partial_total.wait_recv()
    folded = partial_send[0].astype(F32)
    for k in range(heads - 1):
        folded = folded + partial_recv[k].astype(F32)
    turned = pltpu.roll(folded, RANK, 1)
    for j in range(LIVE):
        row = j * TOKENS
        half = folded if row < FOLD else turned
        row = row if row < FOLD else row - FOLD
        blocks32[j] = half[row:row + TOKENS, :]
    blocks32[LIVE] = jnp.zeros((TOKENS, HEAD), F32)
    for k in range(1, groups):
        origin = lax.rem(me_dp + groups - k, groups)
        for r in range(CAP):
            row = ((k - 1) * CAP + r) * TOKENS
            pieces[row:row + TOKENS, :] = blocks32[tab[origin, CAP + r]]
    for j in range(LIVE):
        stays = tab[groups + 2, j].astype(F32)
        pieces[(slots + j) * TOKENS:(slots + j + 1) * TOKENS, :] = blocks32[j] * stays
    own_lane = lax.broadcasted_iota(jnp.int32, pieces.shape, 1)
    grads = pieces[...]
    doubled = jnp.where(own_lane < RANK, grads, pltpu.roll(grads, RANK, 1)).astype(BF16)
    down = lax.dot_general(doubled[:slots * TOKENS], moved_rows, tn, preferred_element_type=F32)
    down = down + lax.dot_general(doubled[slots * TOKENS:], feat_staying[...], tn, preferred_element_type=F32)
    down = down.T
    fold_lane = lax.broadcasted_iota(jnp.int32, (FOLD, HEAD), 1)
    for h in range(heads):
        first = down[h * ROWS:h * ROWS + FOLD, :]
        second = jnp.concatenate(
            [down[h * ROWS + FOLD:(h + 1) * ROWS, :], jnp.zeros((2 * FOLD - ROWS, HEAD), F32)], axis=0
        )
        down_send[h] = jnp.where(fold_lane < RANK, first, second).astype(BF16)

    def send_down(k, carry):
        peer = lax.rem(me_seq + k, heads)
        seq_copy(peer, down_send.at[peer], down_recv.at[k - 1], 1).start()
        return carry

    lax.fori_loop(1, heads, send_down, 0)

    dp_total(up_recv, 1).wait_recv()
    up_sum = up_send[me_dp]
    for k in range(groups - 1):
        up_sum = up_sum + up_recv[k]
    total_send[...] = up_sum * scale

    def send_total(k, carry):
        dp_copy(lax.rem(me_dp + k, groups), total_send, total_recv.at[k - 1], 2).start()
        return carry

    lax.fori_loop(1, groups, send_total, 0)
    gathered = jnp.zeros((ROWS, HEAD), F32)
    row = lax.broadcasted_iota(jnp.int32, (ROWS, HEAD), 0)
    for k in range(heads):
        owner = (me_seq - k) & (heads - 1)
        column = owner * TOKENS + (row & 3)
        gathered = gathered + jnp.where(lane80 == column, logs[k * ROWS:(k + 1) * ROWS, :], 0.0)
    pick = lax.broadcasted_iota(jnp.int32, log_ref.shape[:1] + (ROWS,), 1) >> 2
    pick = (pick == lax.broadcasted_iota(jnp.int32, pick.shape, 0)).astype(F32)
    log_ref[...] = jnp.dot(pick, gathered, preferred_element_type=F32, precision=lax.Precision.HIGHEST)
    dp_total(total_recv, 2).wait_recv()
    whole32[me_dp] = total_send[...]
    for k in range(1, groups):
        whole32[lax.rem(me_dp + groups - k, groups)] = total_recv[k - 1]
    for d in range(groups):
        up_out[d * up_rows:(d + 1) * up_rows, :] = whole32[d, 0:up_rows, :]

    down_total = seq_copy(lax.rem(me_seq + 1, heads), down_send.at[pl.ds(0, heads - 1)], down_recv, 1)
    down_total.wait_recv()
    share = down_send[me_seq].astype(F32)
    for k in range(heads - 1):
        share = share + down_recv[k].astype(F32)
    share_recv[0] = share.astype(BF16)

    def send_share(k, carry):
        dp_copy(lax.rem(me_dp + k, groups), share_recv.at[0], share_recv.at[k], 3).start()
        return carry

    lax.fori_loop(1, groups, send_share, 0)
    share_total = dp_total(share_recv.at[pl.ds(1, groups - 1)], 3)
    share_total.wait_recv()
    share = jnp.zeros((FOLD, HEAD), F32)
    for d in range(groups):
        share = share + share_recv[lax.rem(me_dp + groups - d, groups)].astype(F32)
    share = share * scale
    turned = pltpu.roll(share, RANK, 1)
    whole = jnp.concatenate(
        [share, turned[:ROWS - FOLD], jnp.zeros((HEAD - ROWS, HEAD), F32)], axis=0
    )
    down_out[...] = whole.T[:RANK, :ROWS]

    dp_total(feat_recv, 0).wait_send()
    dp_total(up_recv, 1).wait_send()
    dp_total(total_recv, 2).wait_send()
    share_total.wait_send()
    partial_total.wait_send()
    down_total.wait_send()
    for part in range(parts):
        dp_part(keys_send.at[part], keys_pool[part], part).wait_send()
        dp_part(query_send.at[part], query_pool[part], parts + part).wait_send()
        dp_part(values_send.at[part], values_pool[part], 2 * parts + part).wait_send()
    dp_part(adapter_send, adapter_pool, 3 * parts).wait_send()
    for index, got in enumerate((keys_got, values_got, query_got, grad_got, adapter_got)):
        seq_total(got, index).wait_send()


def whole(tables, segments, down_t, up, keys, values, base, grads, features, scale, groups, heads):
    blocks = keys.shape[0]
    slots = (groups - 1) * CAP
    width = heads * HEAD
    total = heads * ROWS
    parts = min(PARTS, heads)
    inputs = features.shape[2]
    vmem = pl.BlockSpec(memory_space=pltpu.VMEM)
    hbm = pl.BlockSpec(memory_space=pl.ANY)
    up_tile = max(8, RANK // groups)

    def array(*shape, dtype=BF16):
        return pltpu.VMEM(shape, dtype)

    def numbers(*shape):
        return pltpu.VMEM(shape, F32)

    arriving = array(slots, TOKENS, width // parts)
    moving = array(parts, slots, TOKENS, width // parts)
    here = array(blocks, TOKENS, width)
    chunks = array(heads, ROWS, HEAD)
    folded = array(heads, FOLD, HEAD)
    received = array(heads - 1, FOLD, HEAD)
    return pl.pallas_call(
        functools.partial(whole_kernel, groups, heads, parts, scale),
        out_shape=(
            jax.ShapeDtypeStruct((RANK, ROWS), F32),
            jax.ShapeDtypeStruct((RANK, HEAD), F32),
            jax.ShapeDtypeStruct((blocks, HEAD), F32),
        ),
        in_specs=[pl.BlockSpec(memory_space=pltpu.SMEM)] + [vmem] * 3 + [hbm] * 5,
        out_specs=[vmem] * 3,
        scratch_shapes=[arriving] * (3 * parts) + [
            array(slots, TOKENS, HEAD),
            here, here, here, array(blocks, TOKENS, HEAD), here, array(blocks, TOKENS, inputs),
            moving, moving, moving, array(slots, TOKENS, HEAD),
            chunks, chunks, chunks, chunks, array(FOLD, HEAD),
            numbers(ROWS, width),
            numbers(max(slots, blocks) * TOKENS, inputs),
            numbers(blocks * TOKENS, width),
            numbers(max(blocks * TOKENS, 2 * FOLD), HEAD),
            chunks, chunks, chunks, chunks, folded,
            array(groups - 1, CAP * TOKENS, inputs), array(ROWS, inputs),
            array(total, HEAD), array(total, HEAD), array(total, 2 * HEAD), array(total, 2 * HEAD),
            numbers(total // parts, total), array(total, total), array(total, HEAD), numbers(total, HEAD),
            array(RANK, HEAD),
            array(groups - 1, CAP * TOKENS, inputs),
            folded, received,
            numbers(LIVE + 1, TOKENS, HEAD), numbers((slots + LIVE) * TOKENS, HEAD),
            folded, received,
            numbers(groups, up_tile, HEAD), numbers(groups - 1, up_tile, HEAD),
            numbers(up_tile, HEAD), numbers(groups - 1, up_tile, HEAD), numbers(groups, up_tile, HEAD),
            array(groups, FOLD, HEAD),
            pltpu.SemaphoreType.DMA,
            pltpu.SemaphoreType.DMA((5,)),
            pltpu.SemaphoreType.DMA((5,)),
            pltpu.SemaphoreType.DMA((3 * parts + 5,)),
            pltpu.SemaphoreType.DMA((3 * parts + 5,)),
            pltpu.SemaphoreType.DMA((7,)),
            pltpu.SemaphoreType.DMA((7,)),
        ],
        compiler_params=pltpu.CompilerParams(
            collective_id=1, has_side_effects=True, vmem_limit_bytes=VMEM_LIMIT
        ),
        name="whole",
    )(tables, segments, down_t, up, keys, values, base, grads, features)


def per_device(
    features, frozen_query_weight, source_keys, source_values, output_gradient,
    adapter_down_weight, adapter_up_weight, source_block_plan, segments,
):
    groups = lax.axis_size("dp")
    heads = lax.axis_size("seq")
    length = segments.shape[1]
    tables = block_tables(source_block_plan, groups)
    scale = 4.0 / math.sqrt(groups * length)
    down, up, logs = whole(
        tables, segments, adapter_down_weight.T, adapter_up_weight, source_keys[0], source_values[0],
        frozen_query_weight[0], output_gradient[0], features[0], scale, groups, heads,
    )
    log_norm = logs[:, : TOKENS * heads].reshape(1, 1, length)
    return (down.T, up, log_norm)


def solution(mesh):
    in_specs = (
        P("dp", None, "seq", None),
        P("dp", None, "seq", None),
        P("dp", None, "seq", None),
        P("dp", None, "seq", None),
        P("dp", None, "seq", None),
        P(),
        P(),
        P(),
        P("dp", None),
    )
    out_specs = (P("seq", None), P(None, "seq"), P("dp", "seq", None))
    return jax.shard_map(
        per_device, mesh=mesh, in_specs=in_specs, out_specs=out_specs, check_vma=False
    )
```

time: 160 us -> 143 us (0.89)
  Pallas kernels: 157 us -> 139 us
    pallas_call x2 -> x1, Pallas kernels: 155 us -> 138 us  [whole(): pl.pallas_call(functools.partial(whole_kernel, groups, heads, parts, scal...]
where the time goes in v3:
time: 143 us; the launch traced here: 142 us
  Pallas kernels  139 us (97%)
  local copies, waits for them, and re-layouts  2.72 us (2%)
    pallas_call x1, Pallas kernels, whole(): pl.pallas_call(functools.partial(whole_kernel, groups, heads, parts, scal...  138 us

profile of v3, /device:TPU:1, one launch (start us, length us, event | category | flops | bytes accessed | tf_op | source)
XLA Modules:
  0.0 142.4 jit_solution(13817972887796506302)
XLA Ops:
  0.6 1.5 %tables.1.tab = s32[24,128]{1,0:T(8,128)} custom-call(s32[16,32]{1,0:T(8,128)} %plan_ref.1), custom_call_target="tpu_custom_call" | custom-call | tf_op jit(solution)/shard_map/tables/pallas_call | solution.py:64
  2.1 137.5 %whole.1 = (f32[64,80]{1,0:T(8,128)}, f32[64,128]{1,0:T(8,128)}, f32[32,128]{1,0:T(8,128)}) custom-call(s32[24,128]{1,0:T(8,128)} %tables.1.tab, s32[1,4096]{1,0:T(1,128)} %segments_ref.1, bf16[64,2560]{1,0:T(8,128)(2,1)} %bitcast.13, bf16[64,4096]{1,0:T(8,128)(2,1)} %up_ref.1, bf16[32,4,4096]{2,1,0:T(4,128)(2,1)} %bitcast.8, bf16[32,4,4096]{2,1,0:T(4,128)(2,1)} %bitcast.9, ...), custom_call_target="tpu_custom_call" | custom-call | tf_op jit(solution)/shard_map/whole/pallas_call | solution.py:596
  139.7 0.0 copy-start
  139.7 1.4 copy.15
  141.1 0.0 copy-done
  141.1 0.0 copy-start.1
  141.1 0.6 copy.16
  141.7 0.1 copy-done.1
  141.8 0.6 copy.17
Async XLA Ops:
  139.7 1.4 copy-start
  141.1 0.7 copy-start.1

commit v4 on v3

--- a/solution.py
+++ b/solution.py
@@ -90,6 +90,11 @@
     return barrier
 
 
+def seq_shape(heads):
+    across = 4 if heads >= 8 else heads // 2
+    return across, heads // across
+
+
 def whole_kernel(
     groups, heads, parts, scale, tab, segments_ref, down_ref, up_ref, keys_in, values_in, base_in, grad_in, feat_in,
     down_out, up_out, log_ref,
@@ -101,9 +106,9 @@
         keys_here, values_here, query_here, adapter_here, grad_buf, feat_buf,
         keys_send, values_send, query_send, adapter_send,
         keys_stage, values_stage, query_stage, grad_stage, adapter_stage, rows32, feat32, up32, adapter32,
-        keys_got, values_got, query_got, grad_got, adapter_got, feat_moving, feat_staying,
+        keys_got, values_got, query_got, grad_got, adapter_got, feat_moving, feat_turned,
         key_max, key_sum, value_sum, value_neg, scores, probs, dquery, logs, up_head,
-        feat_recv, partial_send, partial_recv, blocks32, pieces, down_send, down_recv,
+        feat_recv, partial_send, partial_recv, blocks32, pieces, down_send, down_x, down_row, down_y,
         up_send, up_recv, total_send, total_recv, whole32, share_recv,
         up_sem, load_sem, own_sem, z_send, z_recv, s_send, s_recv,
     ) = scratch[3 * parts:]
@@ -112,11 +117,14 @@
     slots = (groups - 1) * CAP
     blocks = keys_in.shape[0]
     total = heads * ROWS
-    tile = total // parts
+    tiles = min(4, heads)
+    tile = total // tiles
     step = 256 if total % 256 == 0 else total
     per_tile = tile // ROWS
+    stay_row = feat32.shape[0] - HEAD
     up_rows = RANK // groups
     seq_base = 5
+    rows_x, rows_y = seq_shape(heads)
     dp_base = 3 * parts + 1
     scaling = 1.0 / math.sqrt(HEAD)
     to_exp2 = scaling * math.log2(math.e)
@@ -146,13 +154,12 @@
     )
     up_copy.start()
 
-    def pack(here, send):
+    def pack(here, send, part):
         for i in range(slots):
-            block = here[slot_source(i)]
-            for part in range(parts):
-                for c in range(per_part):
-                    h = head_of(part, c)
-                    send[part, i, :, c * HEAD:(c + 1) * HEAD] = block[:, h * HEAD:(h + 1) * HEAD]
+            block = slot_source(i)
+            for c in range(per_part):
+                h = head_of(part, c)
+                send[part, i, :, c * HEAD:(c + 1) * HEAD] = here[block, :, h * HEAD:(h + 1) * HEAD]
 
     def send_dp(send, pool, index):
         def one(k, carry):
@@ -230,9 +237,11 @@
         send_part(stage, out, index, part)
 
     loads[0].wait()
-    pack(keys_here, keys_send)
+    pack(keys_here, keys_send, 0)
     pl.semaphore_wait(barrier, groups + heads - 2)
     for part in range(parts):
+        if part > 0:
+            pack(keys_here, keys_send, part)
         send_dp(keys_send.at[part], keys_pool[part], part)
 
     loads[3].wait()
@@ -254,24 +263,26 @@
     for b in range(blocks):
         query_here[b] = (query_here[b].astype(F32) + up32[b * TOKENS:(b + 1) * TOKENS, :]).astype(BF16)
         adapter_here[b] = adapter32[b * TOKENS:(b + 1) * TOKENS, :].astype(BF16)
-    pack(query_here, query_send)
     for i in range(slots):
         adapter_send[i] = adapter_here[slot_source(i)]
     send_dp(adapter_send, adapter_pool, 3 * parts)
     for part in range(parts):
+        pack(query_here, query_send, part)
         send_dp(query_send.at[part], query_pool[part], parts + part)
     loads[4].wait()
-    pack(values_here, values_send)
     for part in range(parts):
+        pack(values_here, values_send, part)
         send_dp(values_send.at[part], values_pool[part], 2 * parts + part)
 
     for i in range(slots):
         feat32[i * TOKENS:(i + 1) * TOKENS, :] = feat_buf[slot_source(i)].astype(F32)
     for k in range(groups - 1):
         feat_moving[k] = feat32[k * CAP * TOKENS:(k + 1) * CAP * TOKENS, :].astype(BF16)
+    feat32[...] = jnp.zeros_like(feat32)
+    pieces[...] = jnp.zeros_like(pieces)
     for j in range(LIVE):
-        feat32[j * TOKENS:(j + 1) * TOKENS, :] = feat_buf[tab[groups + 1, j]].astype(F32)
-    feat_staying[...] = feat32[:ROWS, :].astype(BF16)
+        row = stay_row + j * TOKENS
+        feat32[row:row + TOKENS, :] = feat_buf[tab[groups + 1, j]].astype(F32)
 
     def take_part(send, pool, here, stage, got, index, order, part):
         dp_part(send.at[part], pool[part], order * parts + part).wait_recv()
@@ -358,12 +369,13 @@
 
     for part in range(parts):
         take_part(values_send, values_pool, values_here, values_stage, values_got, 1, 2, part)
-        if part == 0:
+        if part == parts // tiles - 1:
             seq_total(query_got, 2).wait_recv()
             pltpu.make_async_copy(query_stage.at[0], query_got.at[0], own_sem.at[2]).wait()
         if part == parts - 1:
             lax.fori_loop(1, groups, send_features, 0)
-        score_tile(part)
+        if (part + 1) % (parts // tiles) == 0:
+            score_tile(part // (parts // tiles))
 
     up_copy.wait()
     up = up_head[...]
@@ -383,7 +395,7 @@
         value_sum[at, 0:HEAD] = value
         value_neg[at, 0:HEAD] = value
 
-    state = [dict() for _ in range(parts)]
+    state = [dict() for _ in range(tiles)]
 
     def attend_step(t, c):
         own = state[t]
@@ -428,9 +440,9 @@
                         lax.rem(me_seq + heads - k, heads), partial_send.at[k], partial_recv.at[k - 1], 0
                     ).start()
 
-    for t in range(parts + 1):
+    for t in range(tiles + 1):
         for c in range(0, total, step):
-            if t < parts:
+            if t < tiles:
                 attend_step(t, c)
             if t > 0:
                 gradient_step(t - 1, c)
@@ -461,7 +473,7 @@
     dp_total(feat_recv, 0).wait_recv()
     for k in range(groups - 1):
         feat32[k * CAP * TOKENS:(k + 1) * CAP * TOKENS, :] = feat_recv[k].astype(F32)
-    moved_rows = feat32[: slots * TOKENS, :].astype(BF16)
+    feat_turned[...] = feat32[...].T.astype(BF16)
 
     partial_total = seq_copy(lax.rem(me_seq + 1, heads), partial_send.at[pl.ds(1, heads - 1)], partial_recv, 0)
     partial_total.wait_recv()
@@ -482,27 +494,27 @@
             pieces[row:row + TOKENS, :] = blocks32[tab[origin, CAP + r]]
     for j in range(LIVE):
         stays = tab[groups + 2, j].astype(F32)
-        pieces[(slots + j) * TOKENS:(slots + j + 1) * TOKENS, :] = blocks32[j] * stays
+        row = stay_row + j * TOKENS
+        pieces[row:row + TOKENS, :] = blocks32[j] * stays
     own_lane = lax.broadcasted_iota(jnp.int32, pieces.shape, 1)
     grads = pieces[...]
     doubled = jnp.where(own_lane < RANK, grads, pltpu.roll(grads, RANK, 1)).astype(BF16)
-    down = lax.dot_general(doubled[:slots * TOKENS], moved_rows, tn, preferred_element_type=F32)
-    down = down + lax.dot_general(doubled[slots * TOKENS:], feat_staying[...], tn, preferred_element_type=F32)
-    down = down.T
+    down = jnp.dot(feat_turned[...], doubled, preferred_element_type=F32)
     fold_lane = lax.broadcasted_iota(jnp.int32, (FOLD, HEAD), 1)
     for h in range(heads):
         first = down[h * ROWS:h * ROWS + FOLD, :]
         second = jnp.concatenate(
             [down[h * ROWS + FOLD:(h + 1) * ROWS, :], jnp.zeros((2 * FOLD - ROWS, HEAD), F32)], axis=0
         )
-        down_send[h] = jnp.where(fold_lane < RANK, first, second).astype(BF16)
-
-    def send_down(k, carry):
-        peer = lax.rem(me_seq + k, heads)
-        seq_copy(peer, down_send.at[peer], down_recv.at[k - 1], 1).start()
-        return carry
-
-    lax.fori_loop(1, heads, send_down, 0)
+        down_send[h % rows_x, h // rows_x] = jnp.where(fold_lane < RANK, first, second).astype(BF16)
+    me_x, me_y = lax.rem(me_seq, rows_x), me_seq // rows_x
+
+    def send_down_x(k, carry):
+        peer = lax.rem(me_x + k, rows_x)
+        seq_copy(me_y * rows_x + peer, down_send.at[peer], down_x.at[k - 1], 1).start()
+        return carry
+
+    lax.fori_loop(1, rows_x, send_down_x, 0)
 
     dp_total(up_recv, 1).wait_recv()
     up_sum = up_send[me_dp]
@@ -524,6 +536,20 @@
     pick = lax.broadcasted_iota(jnp.int32, log_ref.shape[:1] + (ROWS,), 1) >> 2
     pick = (pick == lax.broadcasted_iota(jnp.int32, pick.shape, 0)).astype(F32)
     log_ref[...] = jnp.dot(pick, gathered, preferred_element_type=F32, precision=lax.Precision.HIGHEST)
+    down_x_total = seq_copy(lax.rem(me_seq + 1, heads), down_x, down_x, 1)
+    down_x_total.wait_recv()
+    for row in range(rows_y):
+        share = down_send[me_x, row].astype(F32)
+        for k in range(rows_x - 1):
+            share = share + down_x[k, row].astype(F32)
+        down_row[row] = share.astype(BF16)
+
+    def send_down_y(k, carry):
+        peer = lax.rem(me_y + k, rows_y)
+        seq_copy(peer * rows_x + me_x, down_row.at[peer], down_y.at[k - 1], 2).start()
+        return carry
+
+    lax.fori_loop(1, rows_y, send_down_y, 0)
     dp_total(total_recv, 2).wait_recv()
     whole32[me_dp] = total_send[...]
     for k in range(1, groups):
@@ -531,11 +557,11 @@
     for d in range(groups):
         up_out[d * up_rows:(d + 1) * up_rows, :] = whole32[d, 0:up_rows, :]
 
-    down_total = seq_copy(lax.rem(me_seq + 1, heads), down_send.at[pl.ds(0, heads - 1)], down_recv, 1)
-    down_total.wait_recv()
-    share = down_send[me_seq].astype(F32)
-    for k in range(heads - 1):
-        share = share + down_recv[k].astype(F32)
+    down_y_total = seq_copy(lax.rem(me_seq + 1, heads), down_y, down_y, 2)
+    down_y_total.wait_recv()
+    share = down_row[me_y].astype(F32)
+    for k in range(rows_y - 1):
+        share = share + down_y[k].astype(F32)
     share_recv[0] = share.astype(BF16)
 
     def send_share(k, carry):
@@ -560,7 +586,8 @@
     dp_total(total_recv, 2).wait_send()
     share_total.wait_send()
     partial_total.wait_send()
-    down_total.wait_send()
+    down_x_total.wait_send()
+    down_y_total.wait_send()
     for part in range(parts):
         dp_part(keys_send.at[part], keys_pool[part], part).wait_send()
         dp_part(query_send.at[part], query_pool[part], parts + part).wait_send()
@@ -580,6 +607,8 @@
     vmem = pl.BlockSpec(memory_space=pltpu.VMEM)
     hbm = pl.BlockSpec(memory_space=pl.ANY)
     up_tile = max(8, RANK // groups)
+    feat_rows = -(-max(slots, blocks) * TOKENS // HEAD) * HEAD + HEAD
+    rows_x, rows_y = seq_shape(heads)
 
     def array(*shape, dtype=BF16):
         return pltpu.VMEM(shape, dtype)
@@ -608,18 +637,19 @@
             moving, moving, moving, array(slots, TOKENS, HEAD),
             chunks, chunks, chunks, chunks, array(FOLD, HEAD),
             numbers(ROWS, width),
-            numbers(max(slots, blocks) * TOKENS, inputs),
+            numbers(feat_rows, inputs),
             numbers(blocks * TOKENS, width),
             numbers(max(blocks * TOKENS, 2 * FOLD), HEAD),
             chunks, chunks, chunks, chunks, folded,
-            array(groups - 1, CAP * TOKENS, inputs), array(ROWS, inputs),
+            array(groups - 1, CAP * TOKENS, inputs), array(inputs, feat_rows),
             array(total, HEAD), array(total, HEAD), array(total, 2 * HEAD), array(total, 2 * HEAD),
-            numbers(total // parts, total), array(total, total), array(total, HEAD), numbers(total, HEAD),
+            numbers(total // min(4, heads), total), array(total, total), array(total, HEAD), numbers(total, HEAD),
             array(RANK, HEAD),
             array(groups - 1, CAP * TOKENS, inputs),
             folded, received,
-            numbers(LIVE + 1, TOKENS, HEAD), numbers((slots + LIVE) * TOKENS, HEAD),
-            folded, received,
+            numbers(LIVE + 1, TOKENS, HEAD), numbers(feat_rows, HEAD),
+            array(rows_x, rows_y, FOLD, HEAD), array(rows_x - 1, rows_y, FOLD, HEAD),
+            array(rows_y, FOLD, HEAD), array(rows_y - 1, FOLD, HEAD),
             numbers(groups, up_tile, HEAD), numbers(groups - 1, up_tile, HEAD),
             numbers(up_tile, HEAD), numbers(groups - 1, up_tile, HEAD), numbers(groups, up_tile, HEAD),
             array(groups, FOLD, HEAD),
@@ -628,8 +658,8 @@
             pltpu.SemaphoreType.DMA((5,)),
             pltpu.SemaphoreType.DMA((3 * parts + 5,)),
             pltpu.SemaphoreType.DMA((3 * parts + 5,)),
-            pltpu.SemaphoreType.DMA((7,)),
-            pltpu.SemaphoreType.DMA((7,)),
+            pltpu.SemaphoreType.DMA((8,)),
+            pltpu.SemaphoreType.DMA((8,)),
         ],
         compiler_params=pltpu.CompilerParams(
             collective_id=1, has_side_effects=True, vmem_limit_bytes=VMEM_LIMIT

time: 143 us -> 142 us (level)
  no operation moved by 1% of the time
where the time goes in v4:
time: 142 us; the launch traced here: 141 us
  Pallas kernels  138 us (97%)
  local copies, waits for them, and re-layouts  2.72 us (2%)
    pallas_call x1, Pallas kernels, whole(): pl.pallas_call(functools.partial(whole_kernel, groups, heads, parts, scal...  136 us

profile of v4, /device:TPU:1, one launch (start us, length us, event | category | flops | bytes accessed | tf_op | source)
XLA Modules:
  0.0 141.3 jit_solution(6150442633901628504)
XLA Ops:
  0.6 1.5 %tables.1.tab = s32[24,128]{1,0:T(8,128)} custom-call(s32[16,32]{1,0:T(8,128)} %plan_ref.1), custom_call_target="tpu_custom_call" | custom-call | tf_op jit(solution)/shard_map/tables/pallas_call | solution.py:64
  2.1 136.5 %whole.1 = (f32[64,80]{1,0:T(8,128)}, f32[64,128]{1,0:T(8,128)}, f32[32,128]{1,0:T(8,128)}) custom-call(s32[24,128]{1,0:T(8,128)} %tables.1.tab, s32[1,4096]{1,0:T(1,128)} %segments_ref.1, bf16[64,2560]{1,0:T(8,128)(2,1)} %bitcast.13, bf16[64,4096]{1,0:T(8,128)(2,1)} %up_ref.1, bf16[32,4,4096]{2,1,0:T(4,128)(2,1)} %bitcast.8, bf16[32,4,4096]{2,1,0:T(4,128)(2,1)} %bitcast.9, ...), custom_call_target="tpu_custom_call" | custom-call | tf_op jit(solution)/shard_map/whole/pallas_call | solution.py:625
  138.6 0.0 copy-start
  138.6 1.4 copy.15
  140.0 0.0 copy-done
  140.0 0.0 copy-start.1
  140.0 0.6 copy.16
  140.6 0.1 copy-done.1
  140.7 0.6 copy.17
Async XLA Ops:
  138.6 1.4 copy-start
  140.0 0.7 copy-start.1
